TPU v7x, 512 devices: a whole 4x8x8 slice. The times are simulated.
512 devices in a mesh: wide: 64 (over x, z, core), narrow: 8 (over y).
Axes of the slice: x: 4, y: 8, z: 8, core: 2. Of those that a mesh axis runs over, the one named last changes fastest.
Arguments:
- positions: float32 [3, 131072], P(None, ('wide', 'narrow')), may hold values from -6 to 6
- velocities: float32 [3, 131072], P(None, ('wide', 'narrow')), may hold values from -4 to 4
- accelerations: float32 [3, 131072], P(None, ('wide', 'narrow')), may hold values from -3 to 3
- jerk_terms: float32 [3, 131072], P(None, ('wide', 'narrow')), may hold values from -6 to 6
- masses: float32 [131072], P(('wide', 'narrow')), may hold values from 7.6293946e-07 to 7.6293945e-05
- levels: int32 [131072], P(('wide', 'narrow')), may hold values from 0 to 3
- active: int32 [4, 4096], P(None, ('wide', 'narrow')), may hold values from 0 to 256, as said below
Outputs:
- new_positions: float32 [3, 131072], P(None, ('wide', 'narrow'))
- new_velocities: float32 [3, 131072], P(None, ('wide', 'narrow'))
- new_accelerations: float32 [3, 131072], P(None, ('wide', 'narrow'))
- new_jerks: float32 [3, 131072], P(None, ('wide', 'narrow'))
- slot_terms: float32 [4, 12, 4096], P(None, None, ('wide', 'narrow'))
Inputs may be any that keep to these rules, and one draw needn't show every extreme that they name: `active`: in each step and block the named stars are distinct and fill the block's first slots; every block names at least one star, and in every step some block fills all 8 slots.
All inputs are finite; a program needn't handle non-finite values.
Results may differ from a plain program's by a relative error of at most 0.0007.
Values sent between devices are 32-bit elements; how exact they have to be, the bound alone decides.
No kernel may reach another device: no remote copies, remote signals or barrier semaphores. Data moves between devices by JAX's collectives and lax.ppermute only.
A program may use at most 64 MiB of HBM per device.

v0:
```python
import math

import jax
import jax.numpy as jnp
from jax import lax
from jax.sharding import PartitionSpec as P

step_size = 1.0 / 32.0
softening = 2.5e-05


def predict(positions, velocities, accelerations, jerk_terms, elapsed):
    ahead_pos = positions + elapsed * (
        velocities + elapsed * (accelerations * 0.5 + elapsed * jerk_terms / 6.0)
    )
    ahead_vel = velocities + elapsed * (accelerations + elapsed * jerk_terms * 0.5)
    return (ahead_pos, ahead_vel)


def pair_sums(targets, source_pos, source_vel, masses):
    delta_x = source_pos[:, None, :] - targets[0:3, :, None]
    delta_v = source_vel[:, None, :] - targets[3:6, :, None]
    radius_sq = jnp.sum(delta_x * delta_x, 0) + softening
    inverse = lax.rsqrt(radius_sq)
    weight = masses[None, :] * inverse * inverse * inverse
    closing = jnp.sum(delta_x * delta_v, 0) / radius_sq
    accel_sum = jnp.sum(weight[None] * delta_x, -1)
    jerk_sum = jnp.sum(weight[None] * (delta_v - 3.0 * closing[None] * delta_x), -1)
    return jnp.concatenate([accel_sum, jerk_sum], 0)


def correct(old_acc, old_jerk, new_acc, new_jerk, interval):
    diff = old_acc - new_acc
    interval_sq = interval * interval
    second = (-6.0 * diff - interval * (4.0 * old_jerk + 2.0 * new_jerk)) / interval_sq
    third = (12.0 * diff + 6.0 * interval * (old_jerk + new_jerk)) / (interval_sq * interval)
    pos_step = interval_sq * interval_sq * (second / 24.0 + interval * third / 120.0)
    vel_step = interval_sq * interval * (second / 6.0 + interval * third / 24.0)
    return (pos_step, vel_step)


def body(positions, velocities, accelerations, jerk_terms, masses, levels, active):
    stars = positions.shape[1]
    slot_count = active.shape[1]
    times = step_size * (1.0 - jnp.exp2(levels.astype(jnp.float32)))
    recorded = []
    for step in range(active.shape[0]):
        block_time = (step + 1) * step_size
        ahead_pos, ahead_vel = predict(
            positions, velocities, accelerations, jerk_terms, block_time - times
        )
        slot_ids = active[step]
        filled = slot_ids < stars
        safe_ids = jnp.minimum(slot_ids, stars - 1)
        own_rows = jnp.concatenate([ahead_pos[:, safe_ids], ahead_vel[:, safe_ids]], 0)
        targets = lax.all_gather(own_rows, ("wide", "narrow"), axis=1, tiled=True)
        total_slots = targets.shape[1]
        block_len = math.gcd(total_slots, 512)
        pieces = targets.reshape(6, total_slots // block_len, block_len).transpose(1, 0, 2)

        def one_block(block):
            return pair_sums(block, ahead_pos, ahead_vel, masses)

        partial_sums = lax.map(one_block, pieces).transpose(1, 0, 2).reshape(6, total_slots)
        summed = lax.psum(partial_sums, ("wide", "narrow"))
        mine = lax.dynamic_slice_in_dim(
            summed, lax.axis_index(("wide", "narrow")) * slot_count, slot_count, 1
        )
        new_acc = mine[0:3]
        new_jerk = mine[3:6]
        interval = block_time - times[safe_ids]
        pos_step, vel_step = correct(
            accelerations[:, safe_ids], jerk_terms[:, safe_ids], new_acc, new_jerk, interval
        )
        new_pos = ahead_pos[:, safe_ids] + pos_step
        new_vel = ahead_vel[:, safe_ids] + vel_step
        stacked = jnp.concatenate([new_acc, new_jerk, pos_step, vel_step], 0)
        recorded.append(jnp.where(filled[None, :], stacked, jnp.zeros_like(stacked)))
        positions = positions.at[:, slot_ids].set(new_pos, mode="drop")
        velocities = velocities.at[:, slot_ids].set(new_vel, mode="drop")
        accelerations = accelerations.at[:, slot_ids].set(new_acc, mode="drop")
        jerk_terms = jerk_terms.at[:, slot_ids].set(new_jerk, mode="drop")
        times = times.at[slot_ids].set(
            jnp.full((slot_count,), block_time, jnp.float32), mode="drop"
        )
    return (positions, velocities, accelerations, jerk_terms, jnp.stack(recorded, 0))


def solution(mesh):
    in_specs = (
        P(None, ("wide", "narrow")),
        P(None, ("wide", "narrow")),
        P(None, ("wide", "narrow")),
        P(None, ("wide", "narrow")),
        P(("wide", "narrow")),
        P(("wide", "narrow")),
        P(None, ("wide", "narrow")),
    )
    out_specs = (
        P(None, ("wide", "narrow")),
        P(None, ("wide", "narrow")),
        P(None, ("wide", "narrow")),
        P(None, ("wide", "narrow")),
        P(None, None, ("wide", "narrow")),
    )
    return jax.shard_map(body, mesh=mesh, in_specs=in_specs, out_specs=out_specs, check_vma=False)
```

profile of v0, /device:TPU:1, one launch (start us, length us, event | category | flops | bytes accessed | tf_op | source)
XLA Modules:
  0.0 1660.8 jit_solution(12239387476865906686)
XLA Ops:
  11.0 119.7 %all_gather.12 = f32[6,4096]{0,1:T(8,128)S(1)} all-gather(f32[6,8]{0,1:T(8,128)S(1)} %pad_maximum_fusion.1), channel_id=1, replica_groups=mesh['wide'=64,'narrow'=8] {'wide','narrow'}, dimensions={1}, use_global_device_ids=true | all-gather | bytes 98496 | tf_op jit(solution)/shard_map/all_gather | solution.py:56
  131.4 12.9 while.40
  132.0 0.9 fusion.145
  133.7 0.9 fusion.145
  135.3 0.9 fusion.145
  136.9 0.9 fusion.145
  138.5 0.9 fusion.145
  140.1 0.9 fusion.145
  141.7 0.9 fusion.145
  143.3 0.9 fusion.145
  144.3 1.9 copy.166
  153.2 268.5 %all-reduce.5.cloned.1.call-done = f32[6,4096]{0,1:T(8,128)} async-done(((f32[6,4096]{0,1:T(8,128)}), f32[6,4096]{0,1:T(8,128)}) %all-reduce.5.cloned.1.call-update) | async-done | bytes 98320 | tf_op jit(solution)/shard_map/psum | solution.py:65
  427.5 110.2 %all_gather.13 = f32[6,4096]{0,1:T(8,128)S(1)} all-gather(f32[6,8]{0,1:T(8,128)S(1)} %pad_maximum_fusion.2), channel_id=1, replica_groups=mesh['wide'=64,'narrow'=8] {'wide','narrow'}, dimensions={1}, use_global_device_ids=true | all-gather | bytes 98496 | tf_op jit(solution)/shard_map/all_gather | solution.py:56
  538.3 12.9 while.41
  539.0 0.9 fusion.148
  540.6 0.9 fusion.148
  542.2 0.9 fusion.148
  543.9 0.9 fusion.148
  545.5 0.9 fusion.148
  547.1 0.9 fusion.148
  548.7 0.9 fusion.148
  550.3 0.9 fusion.148
  551.3 1.9 copy.181
  554.4 275.6 %all-reduce.7.cloned.1.call-done = f32[6,4096]{0,1:T(8,128)} async-done(((f32[6,4096]{0,1:T(8,128)}), f32[6,4096]{0,1:T(8,128)}) %all-reduce.7.cloned.1.call-update) | async-done | bytes 98320 | tf_op jit(solution)/shard_map/psum | solution.py:65
  835.8 110.4 %all_gather.14 = f32[6,4096]{0,1:T(8,128)S(1)} all-gather(f32[6,8]{0,1:T(8,128)S(1)} %pad_maximum_fusion.3), channel_id=1, replica_groups=mesh['wide'=64,'narrow'=8] {'wide','narrow'}, dimensions={1}, use_global_device_ids=true | all-gather | bytes 98496 | tf_op jit(solution)/shard_map/all_gather | solution.py:56
  946.8 12.9 while.42
  947.5 0.9 fusion.151
  949.1 0.9 fusion.151
  950.7 0.9 fusion.151
  952.3 0.9 fusion.151
  954.0 0.9 fusion.151
  955.6 0.9 fusion.151
  957.2 0.9 fusion.151
  958.8 0.9 fusion.151
  959.8 1.9 copy.191
  962.9 275.7 %all-reduce.9.cloned.1.call-done = f32[6,4096]{0,1:T(8,128)} async-done(((f32[6,4096]{0,1:T(8,128)}), f32[6,4096]{0,1:T(8,128)}) %all-reduce.9.cloned.1.call-update) | async-done | bytes 98320 | tf_op jit(solution)/shard_map/psum | solution.py:65
  1244.4 110.2 %all_gather.15 = f32[6,4096]{0,1:T(8,128)S(1)} all-gather(f32[6,8]{0,1:T(8,128)S(1)} %pad_maximum_fusion.4), channel_id=1, replica_groups=mesh['wide'=64,'narrow'=8] {'wide','narrow'}, dimensions={1}, use_global_device_ids=true | all-gather | bytes 98496 | tf_op jit(solution)/shard_map/all_gather | solution.py:56
  1355.2 12.9 while.43
  1355.9 0.9 fusion.154
  1357.5 0.9 fusion.154
  1359.1 0.9 fusion.154
  1360.8 0.9 fusion.154
  1362.4 0.9 fusion.154
  1364.0 0.9 fusion.154
  1365.6 0.9 fusion.154
  1367.2 0.9 fusion.154
  1368.2 1.9 copy.201
  1371.3 275.6 %all-reduce.11.cloned.1.call-done = f32[6,4096]{0,1:T(8,128)} async-done(((f32[6,4096]{0,1:T(8,128)}), f32[6,4096]{0,1:T(8,128)}) %all-reduce.11.cloned.1.call-update) | async-done | bytes 98320 | tf_op jit(solution)/shard_map/psum | solution.py:65
  (276 shorter events, 61.7 us)
Async XLA Ops:
  7.2 414.5 %all-reduce.5.cloned.1.call-start = ((), (), s32[]{:S(2)}) async-start(), calls=%async_computation | async-start | bytes 4194304 | tf_op jit(solution)/shard_map/psum | solution.py:65
  130.7 0.7 copy-start
  146.2 0.7 copy-start.5
  146.2 683.7 %all-reduce.7.cloned.1.call-start = ((), (), s32[]{:S(2)}) async-start(), calls=%async_computation.1 | async-start | bytes 4194304 | tf_op jit(solution)/shard_map/psum | solution.py:65
  148.8 2.6 copy-start.1
  148.9 2.8 copy-start.2
  148.9 2.9 copy-start.3
  148.9 3.0 copy-start.4
  553.2 685.3 %all-reduce.9.cloned.1.call-start = ((), (), s32[]{:S(2)}) async-start(), calls=%async_computation.2 | async-start | bytes 4194304 | tf_op jit(solution)/shard_map/psum | solution.py:65
  961.7 685.2 %all-reduce.11.cloned.1.call-start = ((), (), s32[]{:S(2)}) async-start(), calls=%async_computation.3 | async-start | bytes 4194304 | tf_op jit(solution)/shard_map/psum | solution.py:65
Sparse Core Ops, SparseCore 0:
  146.4 275.2 all-reduce.4
  553.4 276.5 all-reduce.6
  961.8 276.6 all-reduce.8
  1370.2 276.5 all-reduce.10
where the time goes:
time: 1660 us
  waiting for transfers between devices  1100 us (66%)
  blocking collectives  451 us (27%)
  other arithmetic  58.8 us (4%)
  local copies, waits for them, and re-layouts  40.1 us (2%)
    psum x4, waiting for transfers between devices, body(): summed = lax.psum(partial_sums, ('wide', 'narrow'))  1100 us
    all_gather x4, blocking collectives, body(): targets = lax.all_gather(own_rows, ('wide', 'narrow'), axis=1, tiled=True)  451 us
  transfers between devices with their start and end apart: 4, of which 4 were waited for; matrix products, arithmetic and copies ran while one was open for 1% of the time, Pallas kernels for 0%

commit v1 on v0

v1 whole, which is shorter than its diff:
```python
import functools

import jax
import jax.numpy as jnp
from jax import lax
from jax.experimental import pallas as pl
from jax.experimental.pallas import tpu as pltpu
from jax.sharding import Mesh, PartitionSpec as P

step_size = 1.0 / 32.0
softening = 2.5e-05
STEPS = 4
CAP = 8
LANES = 128
HALF = 128
STARS = 256


def predict(x, v, a, j, tau):
    ahead_x = x + tau * (v + tau * (a * 0.5 + tau * j / 6.0))
    ahead_v = v + tau * (a + tau * j * 0.5)
    return ahead_x, ahead_v


def back(x, lanes):
    return pltpu.roll(x, LANES - lanes, 1) if lanes else x


def lane_of(shape):
    return lax.broadcasted_iota(jnp.int32, shape, 1)


def pack_kernel(pos, vel, acc, jerk, mass, levels, active, col_out, row_out, state, rows):
    state[0:3, :] = pos[...]
    state[3:6, :] = vel[...]
    state[6:9, :] = acc[...]
    state[9:12, :] = jerk[...]
    times = step_size * (1.0 - jnp.left_shift(1, levels[...]).astype(jnp.float32))
    state[12:15, :] = jnp.broadcast_to(times, (3, STARS))
    state[15:16, :] = mass[...]
    whole = state[...]
    lane = lane_of((16, LANES))
    diagonal = lane // CAP == lax.broadcasted_iota(jnp.int32, (16, LANES), 0)
    slot = lane % CAP
    star = lane_of((1, STARS))
    for k in range(STEPS):
        table = jnp.zeros((16, LANES), jnp.float32)
        ids = jnp.zeros((1, LANES), jnp.float32)
        for s in range(CAP):
            named = active[k, s]
            column = jnp.sum(jnp.where(star == named, whole, 0.0), axis=1, keepdims=True)
            table = jnp.where(slot == s, column, table)
            ids = jnp.where(slot[0:1] == s, named.astype(jnp.float32), ids)
        rows[k : k + 1, :] = jnp.sum(jnp.where(diagonal, table, 0.0), axis=0, keepdims=True)
        rows[STEPS + k : STEPS + k + 1, :] = ids
    row_out[...] = jnp.broadcast_to(rows[...][None], row_out.shape)
    peers = col_out.shape[0]
    col_out[:, 0:16, :] = jnp.broadcast_to(whole[None, :, :HALF], (peers, 16, HALF))
    col_out[:, 16:32, :] = jnp.broadcast_to(whole[None, :, HALF:], (peers, 16, HALF))


def force_kernel(step, ncol, nrow, *refs):
    block_time = (step + 1) * step_size
    if step == 0:
        raw, target_rows = refs[0], refs[1]
        refs = refs[2:]
    else:
        before, fresh, targets = refs[0], refs[1], refs[2]
        refs = refs[3:]
    if step < STEPS - 1:
        sums_out, state, source, splat, part = refs
    else:
        sums_out, source, splat, part, state = refs

    if step == 0:
        for q in range(14):
            row = 15 if q == 13 else q
            for h in range(2):
                state[q, h * ncol : (h + 1) * ncol, :] = raw[pl.ds(16 * h + row, ncol, stride=32), :]
    else:
        state[...] = before[...]
        changed = fresh[...]
        lane = lane_of((ncol, LANES)).astype(jnp.float32)
        for s in range(CAP):
            named = jnp.broadcast_to(changed[:, 104 + s : 105 + s], (ncol, LANES))
            hits = [named == lane + float(h * HALF) for h in range(2)]
            for q in range(12):
                value = jnp.broadcast_to(changed[:, CAP * q + s : CAP * q + s + 1], (ncol, LANES))
                for h in range(2):
                    at = pl.ds(h * ncol, ncol)
                    state[q, at, :] = jnp.where(hits[h], value, state[q, at, :])
            for h in range(2):
                at = pl.ds(h * ncol, ncol)
                state[12, at, :] = jnp.where(hits[h], step * step_size, state[12, at, :])
    tau = block_time - state[12]
    for c in range(3):
        x, v = predict(state[c], state[3 + c], state[6 + c], state[9 + c], tau)
        source[c] = x
        source[3 + c] = v
    source[6] = state[13]

    z = target_rows[pl.ds(0, nrow, stride=CAP), :] if step == 0 else targets[...]
    x, v = predict(z, back(z, 24), back(z, 48), back(z, 72), block_time - back(z, 96))
    for q in range(6):
        held = x if q < 3 else v
        for s in range(CAP):
            at = CAP * (q % 3) + s
            splat[pl.ds((q * CAP + s) * nrow, nrow), :] = jnp.broadcast_to(
                held[:, at : at + 1], (nrow, LANES)
            )

    count = CAP * nrow
    chunks = 2 * ncol // 8

    def one_target(i, carry):
        g = [jnp.broadcast_to(splat[pl.ds(q * count + i, 1), :], (8, LANES)) for q in range(6)]
        sums = [jnp.zeros((8, LANES), jnp.float32) for _ in range(6)]
        for c in range(chunks):
            at = pl.ds(8 * c, 8)
            dx, dy, dz = (source[q, at, :] - g[q] for q in range(3))
            du, dv, dw = (source[q, at, :] - g[q] for q in range(3, 6))
            radius_sq = (dx * dx + dy * dy + dz * dz) + softening
            inverse = lax.rsqrt(radius_sq)
            inverse_sq = inverse * inverse
            weight = source[6, at, :] * inverse * inverse_sq
            closing = (dx * du + dy * dv + dz * dw) * (3.0 * inverse_sq)
            sums[0] = sums[0] + weight * dx
            sums[1] = sums[1] + weight * dy
            sums[2] = sums[2] + weight * dz
            sums[3] = sums[3] + weight * (du - closing * dx)
            sums[4] = sums[4] + weight * (dv - closing * dy)
            sums[5] = sums[5] + weight * (dw - closing * dz)
        for q in range(6):
            part[pl.ds(q * count + i, 1), :] = jnp.sum(sums[q], axis=0, keepdims=True)
        return carry

    lax.fori_loop(0, count, one_target, 0, unroll=2)

    lane = lane_of((nrow, LANES))
    total = jnp.zeros((nrow, LANES), jnp.float32)
    for q in range(6):
        for s in range(CAP):
            line = part[pl.ds((q * CAP + s) * nrow, nrow), :]
            total = jnp.where(lane == CAP * q + s, jnp.sum(line, axis=1, keepdims=True), total)
    sums_out[...] = jnp.broadcast_to(total[None], sums_out.shape)


def correct(old_acc, old_jerk, new_acc, new_jerk, interval):
    diff = old_acc - new_acc
    interval_sq = interval * interval
    second = (-6.0 * diff - interval * (4.0 * old_jerk + 2.0 * new_jerk)) / interval_sq
    third = (12.0 * diff + 6.0 * interval * (old_jerk + new_jerk)) / (interval_sq * interval)
    pos_step = interval_sq * interval_sq * (second / 24.0 + interval * third / 120.0)
    vel_step = interval_sq * interval * (second / 6.0 + interval * third / 24.0)
    return (pos_step, vel_step)


def turn(x, d, slot):
    if d == 0:
        return x
    return jnp.where(slot < CAP - d, pltpu.roll(x, LANES - d, 1), pltpu.roll(x, CAP - d, 1))


def spread(line, diagonal):
    x = jnp.where(diagonal, jnp.broadcast_to(line, (16, LANES)), 0.0)
    for shift in (64, 32, 16, 8):
        x = x + pltpu.roll(x, shift, 1)
    return x


def correct_kernel(step, nrow, me_of, *refs):
    block_time = (step + 1) * step_size
    gathered, target_rows = refs[0], refs[1]
    refs = refs[2:]
    if step > 0:
        targets, refs = refs[0], refs[1:]
        earlier, refs = refs[:step], refs[step:]
    else:
        earlier = ()
    last = step == STEPS - 1
    if last:
        term_rows, refs = refs[: STEPS - 1], refs[STEPS - 1 :]
        pos, vel, acc, jerk, active = refs[:5]
        new_pos, new_vel, new_acc, new_jerk, terms_out, state, keep = refs[5:]
    else:
        corrected_out, next_out, fresh_out, terms_out, keep = refs
    me = me_of()

    total = gathered[0]
    for p in range(1, nrow):
        total = total + gathered[p]
    z = target_rows[pl.ds(0, nrow, stride=CAP), :] if step == 0 else targets[...]
    ids = target_rows[pl.ds(STEPS + step, nrow, stride=CAP), :]
    lane = lane_of((nrow, LANES))
    slot = lane % CAP
    tau = block_time - back(z, 96)
    old_acc, old_jerk = back(z, 48), back(z, 72)
    x, v = predict(z, back(z, 24), old_acc, old_jerk, tau)
    new_a, new_j = total, back(total, 24)
    pos_step, vel_step = correct(old_acc, old_jerk, new_a, new_j, tau)

    def lay(*parts):
        out = parts[-1]
        for n in reversed(range(len(parts) - 1)):
            piece = pltpu.roll(parts[n], 24 * n, 1) if n else parts[n]
            out = jnp.where(lane < 24 * (n + 1), piece, out)
        return out

    rest = jnp.where(lane < 120, block_time, z)
    corrected = lay(x + pos_step, v + vel_step, new_a, new_j, rest)
    terms = lay(new_a, new_j, pos_step, vel_step, jnp.zeros_like(z))
    terms = jnp.where(ids < float(STARS), terms, 0.0)

    keep[0] = terms
    own_terms = keep[0, pl.ds(me, 1), :]
    if not last:
        terms_out[...] = own_terms
        corrected_out[...] = corrected
        keep[1] = jnp.where((lane >= 104) & (lane < 112), ids, corrected)
        fresh_out[...] = jnp.broadcast_to(keep[1, pl.ds(me, 1), :][None], fresh_out.shape)
        following = target_rows[pl.ds(step + 1, nrow, stride=CAP), :]
        wanted = target_rows[pl.ds(STEPS + step + 1, nrow, stride=CAP), :]
        real = wanted < float(STARS)
        for j in range(step + 1):
            values = earlier[j][...] if j < step else corrected
            names = target_rows[pl.ds(STEPS + j, nrow, stride=CAP), :]
            for d in range(CAP):
                hit = (turn(names, d, slot) == wanted) & real
                following = jnp.where(hit, turn(values, d, slot), following)
        next_out[...] = following
        return

    keep[1] = corrected
    wide_lane = lane_of((16, LANES))
    diagonal = wide_lane // CAP == lax.broadcasted_iota(jnp.int32, (16, LANES), 0)
    state[0:3, :] = pos[...]
    state[3:6, :] = vel[...]
    state[6:9, :] = acc[...]
    state[9:12, :] = jerk[...]
    state[12:16, :] = jnp.zeros((4, STARS), jnp.float32)
    whole = state[...]
    star = lane_of((16, STARS))
    for j in range(STEPS):
        line = earlier[j][pl.ds(me, 1), :] if j < step else keep[1, pl.ds(me, 1), :]
        columns = spread(line, diagonal)
        for s in range(CAP):
            whole = jnp.where(star == active[j, s], columns[:, s : s + 1], whole)
        line = term_rows[j][...] if j < step else own_terms
        terms_out[j] = spread(line, diagonal)[0:12, 0:CAP]
    new_pos[...] = whole[0:3, :]
    new_vel[...] = whole[3:6, :]
    new_acc[...] = whole[6:9, :]
    new_jerk[...] = whole[9:12, :]


def struct(*shape):
    return jax.ShapeDtypeStruct(shape, jnp.float32)


def scratch(*shape):
    return pltpu.VMEM(shape, jnp.float32)


vmem = pl.BlockSpec(memory_space=pltpu.VMEM)
smem = pl.BlockSpec(memory_space=pltpu.SMEM)


def send_all(x, axes):
    return lax.all_to_all(x, axes, split_axis=0, concat_axis=0, tiled=True)


def body(ncol, nrow, narrow, pos, vel, acc, jerk, masses, levels, active):
    def me_of():
        return lax.axis_index("core") * narrow + lax.axis_index("narrow")

    col_block, row_block = pl.pallas_call(
        pack_kernel,
        out_shape=(struct(ncol, 32, LANES), struct(nrow, 8, LANES)),
        in_specs=[vmem] * 6 + [smem],
        out_specs=(vmem, vmem),
        scratch_shapes=[scratch(16, STARS), scratch(8, LANES)],
    )(pos, vel, acc, jerk, masses.reshape(1, STARS), levels.reshape(1, STARS), active)
    target_rows = send_all(row_block, ("core", "narrow")).reshape(nrow * 8, LANES)
    raw = send_all(col_block, "across").reshape(ncol * 32, LANES)

    state = fresh = targets = None
    corrected, terms = [], []
    for step in range(STEPS):
        last = step == STEPS - 1
        operands = (raw, target_rows) if step == 0 else (state, fresh, targets)
        state_shape = (14, 2 * ncol, LANES)
        work = [scratch(7, 2 * ncol, LANES), scratch(48 * nrow, LANES), scratch(48 * nrow, LANES)]
        outs = (struct(nrow, nrow, LANES),)
        if last:
            work.append(scratch(*state_shape))
        else:
            outs += (struct(*state_shape),)
        result = pl.pallas_call(
            functools.partial(force_kernel, step, ncol, nrow),
            out_shape=outs,
            in_specs=[vmem] * len(operands),
            out_specs=(vmem,) * len(outs),
            scratch_shapes=work,
        )(*operands)
        partial_sums = result[0]
        state = None if last else result[1]
        gathered = send_all(partial_sums, ("core", "narrow"))
        operands = [gathered, target_rows]
        if step > 0:
            operands += [targets, *corrected]
        in_specs = [vmem] * len(operands)
        work = [scratch(2, nrow, LANES)]
        if last:
            operands += [*terms, pos, vel, acc, jerk, active]
            in_specs += [vmem] * (STEPS + 3) + [smem]
            outs = (struct(3, STARS),) * 4 + (struct(STEPS, 12, CAP),)
            work = [scratch(16, STARS)] + work
        else:
            outs = (
                struct(nrow, LANES),
                struct(nrow, LANES),
                struct(ncol, 1, LANES),
                struct(1, LANES),
            )
        result = pl.pallas_call(
            functools.partial(correct_kernel, step, nrow, me_of),
            out_shape=outs,
            in_specs=in_specs,
            out_specs=(vmem,) * len(outs),
            scratch_shapes=work,
        )(*operands)
        if last:
            return result
        new_rows, targets, fresh, own_terms = result
        corrected.append(new_rows)
        terms.append(own_terms)
        fresh = send_all(fresh, "across").reshape(ncol, LANES)


def solution(mesh):
    wide, narrow = mesh.shape["wide"], mesh.shape["narrow"]
    ncol, nrow = wide // 2, 2 * narrow
    finer = Mesh(mesh.devices.reshape(ncol, 2, narrow), ("across", "core", "narrow"))
    every = ("across", "core", "narrow")
    in_specs = (P(None, every),) * 4 + (P(every), P(every), P(None, every))
    out_specs = (P(None, every),) * 4 + (P(None, None, every),)
    return jax.shard_map(
        functools.partial(body, ncol, nrow, narrow),
        mesh=finer,
        in_specs=in_specs,
        out_specs=out_specs,
        check_vma=False,
    )
```

time: 1660 us -> 191 us (0.12)
  waiting for transfers between devices: 1100 us -> 0 us
  blocking collectives: 451 us -> 140 us
  other arithmetic: 58.8 us -> 0 us
  Pallas kernels: 0 us -> 48.5 us
  local copies, waits for them, and re-layouts: 40.1 us -> 1.45 us
    psum x4 -> x0, waiting for transfers between devices: 1100 us -> none  [body(): summed = lax.psum(partial_sums, ('wide', 'narrow'))]
    all_gather x4 -> x0, blocking collectives: 451 us -> none  [body(): targets = lax.all_gather(own_rows, ('wide', 'narrow'), axis=1, tiled=True)]
    all_to_all x0 -> x9, blocking collectives: none -> 140 us  [send_all(): return lax.all_to_all(x, axes, split_axis=0, concat_axis=0, tiled=True)]
    pallas_call x0 -> x9, Pallas kernels: none -> 48.5 us  [the longest x4 38.8 us: body(): pl.pallas_call(functools.partial(force_kernel, step, ncol, nrow), out_sha...]
    reduce_sum x64 -> x0, other arithmetic: 44.8 us -> none  [the longest x32 29.6 us: pair_sums(): accel_sum = jnp.sum(weight[None] * delta_x, -1)]
  transfers between devices with their start and end apart: 4 -> 0, of which waited for: 4 -> 0; matrix products, arithmetic and copies ran while one was open for 1% -> 0% of each run, Pallas kernels for 0% -> 0%
where the time goes in v1:
time: 191 us; the launch traced here: 190 us
  blocking collectives  140 us (73%)
  Pallas kernels  48.5 us (25%)
    all_to_all x9, blocking collectives, send_all(): return lax.all_to_all(x, axes, split_axis=0, concat_axis=0, tiled=True)  140 us
    pallas_call x4, Pallas kernels, body(): pl.pallas_call(functools.partial(force_kernel, step, ncol, nrow), out_sha...  38.8 us
    pallas_call x4, Pallas kernels, body(): pl.pallas_call(functools.partial(correct_kernel, step, nrow, me_of), out_...  8.04 us

profile of v1, /device:TPU:1, one launch (start us, length us, event | category | flops | bytes accessed | tf_op | source)
XLA Modules:
  0.0 190.2 jit_solution(7454729257899884848)
XLA Ops:
  0.6 1.7 shard_map.110
  2.4 18.0 %all_to_all.45 = f32[16,8,128]{2,1,0:T(8,128)} all-to-all(f32[16,8,128]{2,1,0:T(8,128)} %get-tuple-element.26), channel_id=1, replica_groups=mesh['across'=32,'core'=2,'narrow'=8] {'core','narrow'}, dimensions={0} | all-to-all | bytes 131072 | tf_op jit(solution)/shard_map/all_to_all | solution.py:269
  20.4 24.9 %all_to_all.46 = f32[32,32,128]{2,1,0:T(8,128)} all-to-all(f32[32,32,128]{2,1,0:T(8,128)} %get-tuple-element.25), channel_id=1, replica_groups=mesh['across'=32,'core'=2,'narrow'=8] {'across'}, dimensions={0} | all-to-all | bytes 1048576 | tf_op jit(solution)/shard_map/all_to_all | solution.py:269
  45.3 9.4 %shard_map.111 = (f32[16,16,128]{2,1,0:T(8,128)}, f32[14,64,128]{2,1,0:T(8,128)}) custom-call(f32[1024,128]{1,0:T(8,128)} %bitcast.12, f32[128,128]{1,0:T(8,128)} %bitcast.7), custom_call_target="tpu_custom_call" | custom-call | tf_op jit(solution)/shard_map/pallas_call | solution.py:298
  54.7 15.4 %all_to_all.47.refs_0_ = f32[16,16,128]{2,1,0:T(8,128)} all-to-all(f32[16,16,128]{2,1,0:T(8,128)} %get-tuple-element.28), channel_id=1, replica_groups=mesh['across'=32,'core'=2,'narrow'=8] {'core','narrow'}, dimensions={0} | all-to-all | bytes 262144 | tf_op jit(solution)/shard_map/all_to_all | solution.py:269
  70.2 1.8 shard_map.112
  71.9 13.6 %all_to_all.48 = f32[32,1,128]{2,1,0:T(1,128)} all-to-all(f32[32,1,128]{2,1,0:T(1,128)} %get-tuple-element.29), channel_id=1, replica_groups=mesh['across'=32,'core'=2,'narrow'=8] {'across'}, dimensions={0} | all-to-all | bytes 32768 | tf_op jit(solution)/shard_map/all_to_all | solution.py:269
  85.5 9.8 %shard_map.113 = (f32[16,16,128]{2,1,0:T(8,128)}, f32[14,64,128]{2,1,0:T(8,128)}) custom-call(f32[14,64,128]{2,1,0:T(8,128)} %get-tuple-element.27.refs_0_, f32[32,128]{1,0:T(8,128)} %bitcast.14, f32[16,128]{1,0:T(8,128)} %get-tuple-element.30.refs_2_), custom_call_target="tpu_custom_call" | custom-call | tf_op jit(solution)/shard_map/pallas_call | solution.py:298
  95.3 14.2 %all_to_all.49.refs_0_ = f32[16,16,128]{2,1,0:T(8,128)} all-to-all(f32[16,16,128]{2,1,0:T(8,128)} %get-tuple-element.32), channel_id=1, replica_groups=mesh['across'=32,'core'=2,'narrow'=8] {'core','narrow'}, dimensions={0} | all-to-all | bytes 262144 | tf_op jit(solution)/shard_map/all_to_all | solution.py:269
  109.5 1.8 shard_map.114
  111.3 13.1 %all_to_all.50 = f32[32,1,128]{2,1,0:T(1,128)} all-to-all(f32[32,1,128]{2,1,0:T(1,128)} %get-tuple-element.34), channel_id=1, replica_groups=mesh['across'=32,'core'=2,'narrow'=8] {'across'}, dimensions={0} | all-to-all | bytes 32768 | tf_op jit(solution)/shard_map/all_to_all | solution.py:269
  124.4 9.8 %shard_map.115 = (f32[16,16,128]{2,1,0:T(8,128)}, f32[14,64,128]{2,1,0:T(8,128)}) custom-call(f32[14,64,128]{2,1,0:T(8,128)} %get-tuple-element.31.refs_0_, f32[32,128]{1,0:T(8,128)} %bitcast.15, f32[16,128]{1,0:T(8,128)} %get-tuple-element.35.refs_2_), custom_call_target="tpu_custom_call" | custom-call | tf_op jit(solution)/shard_map/pallas_call | solution.py:298
  134.1 13.6 %all_to_all.51.refs_0_ = f32[16,16,128]{2,1,0:T(8,128)} all-to-all(f32[16,16,128]{2,1,0:T(8,128)} %get-tuple-element.37), channel_id=1, replica_groups=mesh['across'=32,'core'=2,'narrow'=8] {'core','narrow'}, dimensions={0} | all-to-all | bytes 262144 | tf_op jit(solution)/shard_map/all_to_all | solution.py:269
  147.8 1.9 shard_map.116
  149.6 12.8 %all_to_all.52 = f32[32,1,128]{2,1,0:T(1,128)} all-to-all(f32[32,1,128]{2,1,0:T(1,128)} %get-tuple-element.39), channel_id=1, replica_groups=mesh['across'=32,'core'=2,'narrow'=8] {'across'}, dimensions={0} | all-to-all | bytes 32768 | tf_op jit(solution)/shard_map/all_to_all | solution.py:269
  162.4 9.8 %shard_map.117 = f32[16,16,128]{2,1,0:T(8,128)} custom-call(f32[14,64,128]{2,1,0:T(8,128)} %get-tuple-element.36.refs_0_, f32[32,128]{1,0:T(8,128)} %bitcast.13, f32[16,128]{1,0:T(8,128)} %get-tuple-element.40.refs_2_), custom_call_target="tpu_custom_call" | custom-call | tf_op jit(solution)/shard_map/pallas_call | solution.py:298
  172.3 13.9 %all_to_all.53.refs_0_ = f32[16,16,128]{2,1,0:T(8,128)} all-to-all(f32[16,16,128]{2,1,0:T(8,128)} %shard_map.117), channel_id=1, replica_groups=mesh['across'=32,'core'=2,'narrow'=8] {'core','narrow'}, dimensions={0} | all-to-all | bytes 262144 | tf_op jit(solution)/shard_map/all_to_all | solution.py:269
  186.2 2.6 %shard_map.118 = (f32[3,256]{1,0:T(4,128)}, f32[3,256]{1,0:T(4,128)}, f32[3,256]{1,0:T(4,128)}, f32[3,256]{1,0:T(4,128)}, f32[4,12,8]{2,1,0:T(8,128)}) custom-call(f32[16,16,128]{2,1,0:T(8,128)} %all_to_all.53.refs_0_, f32[128,128]{1,0:T(8,128)} %bitcast.11, f32[16,128]{1,0:T(8,128)} %get-tuple-element.40.refs_2_, f32[16,128]{1,0:T(8,128)} %get-tuple-element.33.refs_3_, ...), custom_call_target="tpu_custom_call" | custom-call | tf_op jit(solution)/shard_map/pallas_call | solution.py:325
  188.8 1.5 copy.16

commit v2 on v1

--- a/solution.py
+++ b/solution.py
@@ -30,7 +30,19 @@
     return lax.broadcasted_iota(jnp.int32, shape, 1)
 
 
-def pack_kernel(pos, vel, acc, jerk, mass, levels, active, col_out, row_out, state, rows):
+def fetch(sources, held, sems):
+    copies = [pltpu.make_async_copy(a, b, sems.at[n]) for n, (a, b) in enumerate(zip(sources, held))]
+    for copy in copies:
+        copy.start()
+    return copies
+
+
+def pack_kernel(*refs):
+    active, col_out, row_out, *held = refs[6:15]
+    state, rows, sems = refs[15:]
+    for copy in fetch(refs[:6], held, sems):
+        copy.wait()
+    pos, vel, acc, jerk, mass, levels = held
     state[0:3, :] = pos[...]
     state[3:6, :] = vel[...]
     state[6:9, :] = acc[...]
@@ -134,14 +146,17 @@
             part[pl.ds(q * count + i, 1), :] = jnp.sum(sums[q], axis=0, keepdims=True)
         return carry
 
-    lax.fori_loop(0, count, one_target, 0, unroll=2)
-
-    lane = lane_of((nrow, LANES))
-    total = jnp.zeros((nrow, LANES), jnp.float32)
+    lax.fori_loop(0, count, one_target, 0, unroll=8)
+
+    half = nrow // 2
+    lane = lane_of((half, LANES))
+    total = jnp.zeros((half, LANES), jnp.float32)
     for q in range(6):
         for s in range(CAP):
-            line = part[pl.ds((q * CAP + s) * nrow, nrow), :]
-            total = jnp.where(lane == CAP * q + s, jnp.sum(line, axis=1, keepdims=True), total)
+            for h in range(2):
+                line = part[pl.ds((q * CAP + s) * nrow + h * half, half), :]
+                line = jnp.sum(line, axis=1, keepdims=True)
+                total = jnp.where(lane == 64 * h + CAP * q + s, line, total)
     sums_out[...] = jnp.broadcast_to(total[None], sums_out.shape)
 
 
@@ -180,8 +195,9 @@
     last = step == STEPS - 1
     if last:
         term_rows, refs = refs[: STEPS - 1], refs[STEPS - 1 :]
-        pos, vel, acc, jerk, active = refs[:5]
-        new_pos, new_vel, new_acc, new_jerk, terms_out, state, keep = refs[5:]
+        started, active = refs[:4], refs[4]
+        new_pos, new_vel, new_acc, new_jerk, terms_out, state, *held, sems, keep = refs[5:]
+        copies = fetch(started, held, sems)
     else:
         corrected_out, next_out, fresh_out, terms_out, keep = refs
     me = me_of()
@@ -189,6 +205,7 @@
     total = gathered[0]
     for p in range(1, nrow):
         total = total + gathered[p]
+    total = jnp.concatenate([total, back(total, 64)], axis=0)
     z = target_rows[pl.ds(0, nrow, stride=CAP), :] if step == 0 else targets[...]
     ids = target_rows[pl.ds(STEPS + step, nrow, stride=CAP), :]
     lane = lane_of((nrow, LANES))
@@ -233,10 +250,10 @@
     keep[1] = corrected
     wide_lane = lane_of((16, LANES))
     diagonal = wide_lane // CAP == lax.broadcasted_iota(jnp.int32, (16, LANES), 0)
-    state[0:3, :] = pos[...]
-    state[3:6, :] = vel[...]
-    state[6:9, :] = acc[...]
-    state[9:12, :] = jerk[...]
+    for copy in copies:
+        copy.wait()
+    for n in range(4):
+        state[3 * n : 3 * n + 3, :] = held[n][...]
     state[12:16, :] = jnp.zeros((4, STARS), jnp.float32)
     whole = state[...]
     star = lane_of((16, STARS))
@@ -246,7 +263,7 @@
         for s in range(CAP):
             whole = jnp.where(star == active[j, s], columns[:, s : s + 1], whole)
         line = term_rows[j][...] if j < step else own_terms
-        terms_out[j] = spread(line, diagonal)[0:12, 0:CAP]
+        terms_out[j] = jnp.transpose(spread(line, diagonal))[0:CAP, 0:12]
     new_pos[...] = whole[0:3, :]
     new_vel[...] = whole[3:6, :]
     new_acc[...] = whole[6:9, :]
@@ -262,7 +279,11 @@
 
 
 vmem = pl.BlockSpec(memory_space=pltpu.VMEM)
+hbm = pl.BlockSpec(memory_space=pltpu.HBM)
 smem = pl.BlockSpec(memory_space=pltpu.SMEM)
+
+
+params = pltpu.CompilerParams(vmem_limit_bytes=8 << 20)
 
 
 def send_all(x, axes):
@@ -270,16 +291,25 @@
 
 
 def body(ncol, nrow, narrow, pos, vel, acc, jerk, masses, levels, active):
+    masses, levels = masses.reshape(1, STARS), levels.reshape(1, STARS)
+    pos, vel, acc, jerk, masses, levels, active = (
+        pltpu.with_memory_space_constraint(a, pltpu.HBM)
+        for a in (pos, vel, acc, jerk, masses, levels, active)
+    )
+
     def me_of():
         return lax.axis_index("core") * narrow + lax.axis_index("narrow")
 
     col_block, row_block = pl.pallas_call(
         pack_kernel,
         out_shape=(struct(ncol, 32, LANES), struct(nrow, 8, LANES)),
-        in_specs=[vmem] * 6 + [smem],
+        in_specs=[hbm] * 6 + [smem],
         out_specs=(vmem, vmem),
-        scratch_shapes=[scratch(16, STARS), scratch(8, LANES)],
-    )(pos, vel, acc, jerk, masses.reshape(1, STARS), levels.reshape(1, STARS), active)
+        scratch_shapes=[scratch(3, STARS)] * 4
+        + [scratch(1, STARS), pltpu.VMEM((1, STARS), jnp.int32)]
+        + [scratch(16, STARS), scratch(8, LANES), pltpu.SemaphoreType.DMA((6,))],
+        compiler_params=params,
+    )(pos, vel, acc, jerk, masses, levels, active)
     target_rows = send_all(row_block, ("core", "narrow")).reshape(nrow * 8, LANES)
     raw = send_all(col_block, "across").reshape(ncol * 32, LANES)
 
@@ -290,7 +320,7 @@
         operands = (raw, target_rows) if step == 0 else (state, fresh, targets)
         state_shape = (14, 2 * ncol, LANES)
         work = [scratch(7, 2 * ncol, LANES), scratch(48 * nrow, LANES), scratch(48 * nrow, LANES)]
-        outs = (struct(nrow, nrow, LANES),)
+        outs = (struct(nrow, nrow // 2, LANES),)
         if last:
             work.append(scratch(*state_shape))
         else:
@@ -301,6 +331,7 @@
             in_specs=[vmem] * len(operands),
             out_specs=(vmem,) * len(outs),
             scratch_shapes=work,
+            compiler_params=params,
         )(*operands)
         partial_sums = result[0]
         state = None if last else result[1]
@@ -312,9 +343,9 @@
         work = [scratch(2, nrow, LANES)]
         if last:
             operands += [*terms, pos, vel, acc, jerk, active]
-            in_specs += [vmem] * (STEPS + 3) + [smem]
-            outs = (struct(3, STARS),) * 4 + (struct(STEPS, 12, CAP),)
-            work = [scratch(16, STARS)] + work
+            in_specs += [vmem] * (STEPS - 1) + [hbm] * 4 + [smem]
+            outs = (struct(3, STARS),) * 4 + (struct(STEPS, CAP, 12),)
+            work = [scratch(16, STARS)] + [scratch(3, STARS)] * 4 + [pltpu.SemaphoreType.DMA((4,))] + work
         else:
             outs = (
                 struct(nrow, LANES),
@@ -328,9 +359,10 @@
             in_specs=in_specs,
             out_specs=(vmem,) * len(outs),
             scratch_shapes=work,
+            compiler_params=params,
         )(*operands)
         if last:
-            return result
+            return (*result[:4], jnp.swapaxes(result[4], 1, 2))
         new_rows, targets, fresh, own_terms = result
         corrected.append(new_rows)
         terms.append(own_terms)

time: 191 us -> 164 us (0.86)
  Pallas kernels: 48.5 us -> 34.7 us
  blocking collectives: 140 us -> 128 us
    all_to_all x9, blocking collectives: 140 us -> 128 us  [send_all(): return lax.all_to_all(x, axes, split_axis=0, concat_axis=0, tiled=True)]
    pallas_call x4, Pallas kernels: 38.8 us -> 29.4 us  [body(): pl.pallas_call(functools.partial(force_kernel, step, ncol, nrow), out_sha...]
    pallas_call x4, Pallas kernels: 8.04 us -> 3.66 us  [body(): pl.pallas_call(functools.partial(correct_kernel, step, nrow, me_of), out_...]
where the time goes in v2:
time: 164 us; the launch traced here: 163 us
  blocking collectives  128 us (78%)
  Pallas kernels  34.7 us (21%)
    all_to_all x9, blocking collectives, send_all(): return lax.all_to_all(x, axes, split_axis=0, concat_axis=0, tiled=True)  128 us
    pallas_call x4, Pallas kernels, body(): pl.pallas_call(functools.partial(force_kernel, step, ncol, nrow), out_sha...  29.4 us
    pallas_call x4, Pallas kernels, body(): pl.pallas_call(functools.partial(correct_kernel, step, nrow, me_of), out_...  3.66 us

profile of v2, /device:TPU:1, one launch (start us, length us, event | category | flops | bytes accessed | tf_op | source)
XLA Modules:
  0.0 163.4 jit_solution(6306229505739641282)
XLA Ops:
  0.6 1.7 %shard_map.110 = (f32[32,32,128]{2,1,0:T(8,128)S(1)}, f32[16,8,128]{2,1,0:T(8,128)S(1)}) custom-call(f32[3,256]{1,0:T(4,128)} %refs_9_.1, f32[3,256]{1,0:T(4,128)} %refs_10_.1, f32[3,256]{1,0:T(4,128)} %refs_11_.1, f32[3,256]{1,0:T(4,128)} %refs_12_.1, f32[1,256]{1,0:T(1,128)} %bitcast.17, s32[1,256]{1,0:T(1,128)} %bitcast.18, s32[4,8]{1,0:T(4,128)} %refs_13_.1), custom_call_target="tpu_custom_call" | custom-call | tf_op jit(solution)/shard_map/pallas_call | solution.py:303
  2.3 16.5 %all_to_all.45 = f32[16,8,128]{2,1,0:T(8,128)S(1)} all-to-all(f32[16,8,128]{2,1,0:T(8,128)S(1)} %get-tuple-element.31), channel_id=1, replica_groups=mesh['across'=32,'core'=2,'narrow'=8] {'core','narrow'}, dimensions={0} | all-to-all | bytes 131072 | tf_op jit(solution)/shard_map/all_to_all | solution.py:290
  18.8 25.8 %all_to_all.46 = f32[32,32,128]{2,1,0:T(8,128)S(1)} all-to-all(f32[32,32,128]{2,1,0:T(8,128)S(1)} %get-tuple-element.30), channel_id=1, replica_groups=mesh['across'=32,'core'=2,'narrow'=8] {'across'}, dimensions={0} | all-to-all | bytes 1048576 | tf_op jit(solution)/shard_map/all_to_all | solution.py:290
  44.7 7.0 %shard_map.111 = (f32[16,8,128]{2,1,0:T(8,128)S(1)}, f32[14,64,128]{2,1,0:T(8,128)S(1)}) custom-call(f32[1024,128]{1,0:T(8,128)S(1)} %bitcast.13, f32[128,128]{1,0:T(8,128)S(1)} %bitcast.8), custom_call_target="tpu_custom_call" | custom-call | tf_op jit(solution)/shard_map/pallas_call | solution.py:328
  51.7 13.6 %all_to_all.47.refs_0_ = f32[16,8,128]{2,1,0:T(8,128)S(1)} all-to-all(f32[16,8,128]{2,1,0:T(8,128)S(1)} %get-tuple-element.33), channel_id=1, replica_groups=mesh['across'=32,'core'=2,'narrow'=8] {'core','narrow'}, dimensions={0} | all-to-all | bytes 131072 | tf_op jit(solution)/shard_map/all_to_all | solution.py:290
  65.3 0.3 shard_map.112
  65.7 13.6 %all_to_all.48 = f32[32,1,128]{2,1,0:T(1,128)S(1)} all-to-all(f32[32,1,128]{2,1,0:T(1,128)S(1)} %get-tuple-element.34), channel_id=1, replica_groups=mesh['across'=32,'core'=2,'narrow'=8] {'across'}, dimensions={0} | all-to-all | bytes 32768 | tf_op jit(solution)/shard_map/all_to_all | solution.py:290
  79.2 7.4 %shard_map.113 = (f32[16,8,128]{2,1,0:T(8,128)S(1)}, f32[14,64,128]{2,1,0:T(8,128)S(1)}) custom-call(f32[14,64,128]{2,1,0:T(8,128)S(1)} %get-tuple-element.32.refs_0_, f32[32,128]{1,0:T(8,128)S(1)} %bitcast.15, f32[16,128]{1,0:T(8,128)S(1)} %get-tuple-element.35.refs_2_), custom_call_target="tpu_custom_call" | custom-call | tf_op jit(solution)/shard_map/pallas_call | solution.py:328
  86.7 11.9 %all_to_all.49.refs_0_ = f32[16,8,128]{2,1,0:T(8,128)S(1)} all-to-all(f32[16,8,128]{2,1,0:T(8,128)S(1)} %get-tuple-element.37), channel_id=1, replica_groups=mesh['across'=32,'core'=2,'narrow'=8] {'core','narrow'}, dimensions={0} | all-to-all | bytes 131072 | tf_op jit(solution)/shard_map/all_to_all | solution.py:290
  98.6 0.3 shard_map.114
  99.0 11.6 %all_to_all.50 = f32[32,1,128]{2,1,0:T(1,128)S(1)} all-to-all(f32[32,1,128]{2,1,0:T(1,128)S(1)} %get-tuple-element.39), channel_id=1, replica_groups=mesh['across'=32,'core'=2,'narrow'=8] {'across'}, dimensions={0} | all-to-all | bytes 32768 | tf_op jit(solution)/shard_map/all_to_all | solution.py:290
  110.6 7.4 %shard_map.115 = (f32[16,8,128]{2,1,0:T(8,128)S(1)}, f32[14,64,128]{2,1,0:T(8,128)S(1)}) custom-call(f32[14,64,128]{2,1,0:T(8,128)S(1)} %get-tuple-element.36.refs_0_, f32[32,128]{1,0:T(8,128)S(1)} %bitcast.16, f32[16,128]{1,0:T(8,128)S(1)} %get-tuple-element.40.refs_2_), custom_call_target="tpu_custom_call" | custom-call | tf_op jit(solution)/shard_map/pallas_call | solution.py:328
  118.0 11.6 %all_to_all.51.refs_0_ = f32[16,8,128]{2,1,0:T(8,128)S(1)} all-to-all(f32[16,8,128]{2,1,0:T(8,128)S(1)} %get-tuple-element.42), channel_id=1, replica_groups=mesh['across'=32,'core'=2,'narrow'=8] {'core','narrow'}, dimensions={0} | all-to-all | bytes 131072 | tf_op jit(solution)/shard_map/all_to_all | solution.py:290
  129.7 0.3 shard_map.116
  130.0 11.6 %all_to_all.52 = f32[32,1,128]{2,1,0:T(1,128)S(1)} all-to-all(f32[32,1,128]{2,1,0:T(1,128)S(1)} %get-tuple-element.44), channel_id=1, replica_groups=mesh['across'=32,'core'=2,'narrow'=8] {'across'}, dimensions={0} | all-to-all | bytes 32768 | tf_op jit(solution)/shard_map/all_to_all | solution.py:290
  141.6 7.5 %shard_map.117 = f32[16,8,128]{2,1,0:T(8,128)S(1)} custom-call(f32[14,64,128]{2,1,0:T(8,128)S(1)} %get-tuple-element.41.refs_0_, f32[32,128]{1,0:T(8,128)S(1)} %bitcast.14, f32[16,128]{1,0:T(8,128)S(1)} %get-tuple-element.45.refs_2_), custom_call_target="tpu_custom_call" | custom-call | tf_op jit(solution)/shard_map/pallas_call | solution.py:328
  149.1 11.6 %all_to_all.53.refs_0_ = f32[16,8,128]{2,1,0:T(8,128)S(1)} all-to-all(f32[16,8,128]{2,1,0:T(8,128)S(1)} %shard_map.117), channel_id=1, replica_groups=mesh['across'=32,'core'=2,'narrow'=8] {'core','narrow'}, dimensions={0} | all-to-all | bytes 131072 | tf_op jit(solution)/shard_map/all_to_all | solution.py:290
  160.7 2.7 %shard_map.118 = (f32[3,256]{1,0:T(4,128)}, f32[3,256]{1,0:T(4,128)}, f32[3,256]{1,0:T(4,128)}, f32[3,256]{1,0:T(4,128)}, f32[4,8,12]{2,1,0:T(8,128)}) custom-call(f32[16,8,128]{2,1,0:T(8,128)S(1)} %all_to_all.53.refs_0_, f32[128,128]{1,0:T(8,128)S(1)} %bitcast.12, f32[16,128]{1,0:T(8,128)S(1)} %get-tuple-element.45.refs_2_, ...), custom_call_target="tpu_custom_call" | custom-call | tf_op jit(solution)/shard_map/pallas_call | solution.py:356

commit v3 on v0

v3 whole, which is shorter than its diff:
```python
import functools

import jax
import jax.numpy as jnp
from jax import lax
from jax.experimental import pallas as pl
from jax.experimental.pallas import tpu as pltpu
from jax.sharding import Mesh, PartitionSpec as P

step_size = 1.0 / 32.0
softening = 2.5e-05
STEPS = 4
CAP = 8
LANES = 128
STARS = 256

NROW = 16
TARGETS = NROW * CAP
GROUPS = TARGETS // 8
AT_ONCE = 8
LIST = TARGETS + 32


def predict(x, v, a, j, tau):
    ahead_x = x + tau * (v + tau * (a * 0.5 + tau * j / 6.0))
    ahead_v = v + tau * (a + tau * j * 0.5)
    return ahead_x, ahead_v


def back(x, lanes):
    return pltpu.roll(x, LANES - lanes, 1) if lanes else x


def lane_of(shape):
    return lax.broadcasted_iota(jnp.int32, shape, 1)


def row_of(shape):
    return lax.broadcasted_iota(jnp.int32, shape, 0)


def turn(x, d):
    if d == 0:
        return x
    slot = lane_of(x.shape) % CAP
    return jnp.where(slot < CAP - d, pltpu.roll(x, LANES - d, 1), pltpu.roll(x, CAP - d, 1))


def fetch(sources, held, sems):
    copies = [pltpu.make_async_copy(a, b, sems.at[n]) for n, (a, b) in enumerate(zip(sources, held))]
    for copy in copies:
        copy.start()
    return copies


def pack_kernel(*refs):
    active, block_out, row_out, state, *held = refs[6:16]
    block, rows, sems = refs[16:]
    for copy in fetch(refs[:6], held, sems):
        copy.wait()
    pos, vel, acc, jerk, mass, levels = held
    for n, part in enumerate((pos, vel, acc, jerk)):
        state[3 * n : 3 * n + 3, :] = part[...]
    times = step_size * (1.0 - jnp.left_shift(1, levels[...]).astype(jnp.float32))
    state[12:15, :] = jnp.broadcast_to(times, (3, STARS))
    state[15:16, :] = mass[...]
    whole = state[...]
    lane = lane_of((1, LANES))
    names = jnp.full((1, LANES), STARS, jnp.int32)
    for k in range(STEPS):
        for s in range(CAP):
            names = jnp.where(lane == CAP * k + s, active[k, s], names)
    block[0:16, :] = whole[:, :LANES]
    block[16:32, :] = whole[:, LANES:]
    block[13:14, :] = names.astype(jnp.float32)
    block_out[...] = jnp.broadcast_to(block[...][None], block_out.shape)
    lane = lane_of((16, LANES))
    diagonal = lane // CAP == row_of((16, LANES))
    slot = lane % CAP
    star = lane_of((1, STARS))
    for k in range(STEPS):
        table = jnp.zeros((16, LANES), jnp.float32)
        names = jnp.zeros((1, LANES), jnp.float32)
        for s in range(CAP):
            named = active[k, s]
            column = jnp.sum(jnp.where(star == named, whole, 0.0), axis=1, keepdims=True)
            table = jnp.where(slot == s, column, table)
            names = jnp.where(slot[0:1] == s, named.astype(jnp.float32), names)
        rows[k : k + 1, :] = jnp.sum(jnp.where(diagonal, table, 0.0), axis=0, keepdims=True)
        rows[STEPS + k : STEPS + k + 1, :] = names
    row_out[...] = jnp.broadcast_to(rows[...][None], row_out.shape)


def plan_kernel(scalars, target_rows, lists, splat):
    for k in range(STEPS):

        def peer(r, n):
            for s in range(CAP):
                lists[k, n] = NROW * s + r
                n = n + jnp.where(scalars[CAP * r + STEPS + k, s] < float(STARS), 1, 0)
            return n

        n = lax.fori_loop(0, NROW, peer, 0)
        for u in range(AT_ONCE):
            lists[k, n + u] = 0
        lists[k, LIST - 1] = n
    spread_targets(target_rows_at(target_rows, 0), splat, step_size)


def predict_sources(raw, source, block_time, ncol):
    for h in range(2):
        at = pl.ds(h * ncol, ncol)

        def load(q):
            return raw[pl.ds(16 * h + q, ncol, stride=32), :]

        tau = block_time - load(12)
        for c in range(3):
            x, v = predict(load(c), load(3 + c), load(6 + c), load(9 + c), tau)
            source[c, at, :] = x
            source[3 + c, at, :] = v


def spread_targets(z, splat, block_time):
    x, v = predict(z, back(z, 24), back(z, 48), back(z, 72), block_time - back(z, 96))
    for q in range(6):
        held = x if q < 3 else v
        for s in range(CAP):
            at = CAP * (q % 3) + s
            splat[pl.ds((q * CAP + s) * NROW, NROW), :] = jnp.broadcast_to(
                held[:, at : at + 1], (NROW, LANES)
            )


def add_pairs(sums, sources, target):
    dx, dy, dz, du, dv, dw = (sources[q] - target[q] for q in range(6))
    radius_sq = (dx * dx + dy * dy + dz * dz) + softening
    inverse = lax.rsqrt(radius_sq)
    inverse_sq = inverse * inverse
    weight = sources[6] * inverse * inverse_sq
    closing = (dx * du + dy * dv + dz * dw) * (3.0 * inverse_sq)
    return (
        sums[0] + weight * dx,
        sums[1] + weight * dy,
        sums[2] + weight * dz,
        sums[3] + weight * (du - closing * dx),
        sums[4] + weight * (dv - closing * dy),
        sums[5] + weight * (dw - closing * dz),
    )


def wide_row(ref, q, r):
    return jnp.broadcast_to(ref[q, pl.ds(r, 1), :], (8, LANES))


def sum_listed(source, splat, part, lists, step):
    chunks = source.shape[1] // 8
    part[...] = jnp.zeros(part.shape, jnp.float32)
    zero = jnp.zeros((8, LANES), jnp.float32)

    def some_targets(n, carry):
        for u in range(AT_ONCE):
            i = lists[step, AT_ONCE * n + u]
            target = [
                jnp.broadcast_to(splat[pl.ds(q * TARGETS + i, 1), :], (8, LANES)) for q in range(6)
            ]
            sums = (zero,) * 6
            for c in range(chunks):
                sums = add_pairs(sums, [source[q, pl.ds(8 * c, 8), :] for q in range(7)], target)
            for q in range(6):
                part[pl.ds(q * TARGETS + i, 1), :] = jnp.sum(sums[q], axis=0, keepdims=True)
        return carry

    lax.fori_loop(0, (lists[step, LIST - 1] + AT_ONCE - 1) // AT_ONCE, some_targets, 0)


def pack_sums(part):
    lane = lane_of((8, LANES))
    total = jnp.zeros((8, LANES), jnp.float32)
    for q in range(6):
        for g in range(GROUPS):
            line = jnp.sum(part[pl.ds(q * TARGETS + 8 * g, 8), :], axis=1, keepdims=True)
            total = jnp.where(lane == 64 * (g % 2) + CAP * q + g // 2, line, total)
    return total


def load_masses(raw, ncol):
    return [raw[pl.ds(16 * h + 15, ncol, stride=32), :] for h in range(2)]


def first_force_kernel(ncol, raw, lists_in, splat, sums_out, lists, sem, source, part):
    copy = pltpu.make_async_copy(lists_in, lists, sem)
    copy.start()
    predict_sources(raw, source, step_size, ncol)
    for h, mass in enumerate(load_masses(raw, ncol)):
        source[6, pl.ds(h * ncol, ncol), :] = mass
    copy.wait()
    sum_listed(source, splat, part, lists, 0)
    sums_out[...] = jnp.broadcast_to(pack_sums(part)[None], sums_out.shape)


def target_rows_at(target_rows, n):
    return target_rows[pl.ds(n, NROW, stride=CAP), :]


def take_over(rows, names, wanted, values):
    real = wanted < float(STARS)
    for d in range(CAP):
        rows = jnp.where((turn(names, d) == wanted) & real, turn(values, d), rows)
    return rows


def static_kernel(step, ncol, *refs):
    raw, lists_in, target_rows = refs[:3]
    corrected, refs = refs[3 : 3 + step], refs[3 + step :]
    total_out, splat, targets, lists, sem, source, part = refs
    block_time = (step + 1) * step_size
    copy = pltpu.make_async_copy(lists_in, lists, sem)
    copy.start()
    rows = target_rows_at(target_rows, step)
    wanted = target_rows_at(target_rows, STEPS + step)
    for j in range(step):
        names = target_rows_at(target_rows, STEPS + j)
        rows = take_over(rows, names, wanted, corrected[j][...])
    targets[...] = rows
    spread_targets(rows, splat, block_time)
    predict_sources(raw, source, block_time, ncol)
    masses = load_masses(raw, ncol)
    names = raw[pl.ds(13, ncol, stride=32), :]
    lane = lane_of((ncol, LANES)).astype(jnp.float32)
    for at in range(CAP * step):
        named = jnp.broadcast_to(names[:, at : at + 1], (ncol, LANES))
        for h in range(2):
            masses[h] = jnp.where(named == lane + float(h * LANES), 0.0, masses[h])
    for h in range(2):
        source[6, pl.ds(h * ncol, ncol), :] = masses[h]
    copy.wait()
    sum_listed(source, splat, part, lists, step)
    total_out[...] = pack_sums(part)


def to_columns(x):
    group = lane_of((16, LANES)) // CAP
    row = row_of((16, LANES))
    out = x
    for d in range(16):
        moved = pltpu.roll(x, CAP * d, 1) if d else x
        moved = pltpu.roll(moved, 16 - d, 0) if d else moved
        out = moved if d == 0 else jnp.where(group == (row + d) % 16, moved, out)
    return out


def fresh_kernel(step, ncol, *refs):
    total_in, splat, fresh, *refs = refs
    if step > 1:
        older, *refs = refs
    sums_out, columns, source = refs
    halves = max(ncol // 16, 1)
    blocks = halves * step
    first = halves * (step - 1)
    for h in range(halves):
        columns[pl.ds(16 * (first + h), 16), :] = to_columns(fresh[pl.ds(16 * h, 16), :])
    if step > 1:
        columns[pl.ds(0, 16 * first), :] = older[...]
        for h in range(halves):
            later = columns[pl.ds(16 * (first + h) + 13, 1), :]
            for j in range(step - 1):
                at = 16 * (halves * j + h)
                names = columns[pl.ds(at + 13, 1), :]
                again = jnp.zeros((1, LANES), jnp.float32)
                for d in range(CAP):
                    again = jnp.where(turn(later, d) == names, 1.0, again)
                mass = columns[pl.ds(at + 15, 1), :]
                columns[pl.ds(at + 15, 1), :] = jnp.where(again > 0.5, 0.0, mass)
    for b in range(blocks):
        tau = (step - b // halves) * step_size

        def load(q):
            return columns[pl.ds(16 * b + q, 1), :]

        for c in range(3):
            x, v = predict(load(c), load(3 + c), load(6 + c), load(9 + c), tau)
            source[c, b : b + 1, :] = x
            source[3 + c, b : b + 1, :] = v
        source[6, b : b + 1, :] = load(15)
    lane = lane_of((8, LANES))
    total = total_in[...]
    zero = jnp.zeros((8, LANES), jnp.float32)
    for g in range(GROUPS):
        target = [splat[pl.ds(q * TARGETS + 8 * g, 8), :] for q in range(6)]
        sums = (zero,) * 6
        for b in range(blocks):
            sums = add_pairs(sums, [wide_row(source, q, b) for q in range(7)], target)
        for q in range(6):
            line = jnp.sum(sums[q], axis=1, keepdims=True)
            total = jnp.where(lane == 64 * (g % 2) + CAP * q + g // 2, total + line, total)
    sums_out[...] = jnp.broadcast_to(total[None], sums_out.shape)


def correct(old_acc, old_jerk, new_acc, new_jerk, interval):
    diff = old_acc - new_acc
    interval_sq = interval * interval
    second = (-6.0 * diff - interval * (4.0 * old_jerk + 2.0 * new_jerk)) / interval_sq
    third = (12.0 * diff + 6.0 * interval * (old_jerk + new_jerk)) / (interval_sq * interval)
    pos_step = interval_sq * interval_sq * (second / 24.0 + interval * third / 120.0)
    vel_step = interval_sq * interval * (second / 6.0 + interval * third / 24.0)
    return (pos_step, vel_step)


def correct_rows(step, gathered, target_rows, targets):
    block_time = (step + 1) * step_size
    total = gathered[0]
    for p in range(1, NROW):
        total = total + gathered[p]
    total = jnp.concatenate([total, back(total, 64)], axis=0)
    z = target_rows_at(target_rows, 0) if step == 0 else targets[...]
    names = target_rows_at(target_rows, STEPS + step)
    lane = lane_of((NROW, LANES))
    tau = block_time - back(z, 96)
    old_acc, old_jerk = back(z, 48), back(z, 72)
    x, v = predict(z, back(z, 24), old_acc, old_jerk, tau)
    new_a, new_j = total, back(total, 24)
    pos_step, vel_step = correct(old_acc, old_jerk, new_a, new_j, tau)

    def lay(*parts):
        out = parts[-1]
        for n in reversed(range(len(parts) - 1)):
            piece = pltpu.roll(parts[n], 24 * n, 1) if n else parts[n]
            out = jnp.where(lane < 24 * (n + 1), piece, out)
        return out

    filled = names < float(STARS)
    rest = jnp.where(lane < 120, block_time, z)
    corrected = lay(x + pos_step, v + vel_step, new_a, new_j, rest)
    terms = lay(new_a, new_j, pos_step, vel_step, jnp.zeros_like(z))
    return jnp.where(filled, corrected, 0.0), jnp.where(filled, terms, 0.0), names


def correct_kernel(step, me_of, *refs):
    gathered, target_rows, *refs = refs
    targets = None
    if step > 0:
        targets, *refs = refs
    corrected_out, fresh_out, terms_out, keep = refs
    me = me_of()
    corrected, terms, names = correct_rows(step, gathered, target_rows, targets)
    lane = lane_of((NROW, LANES))
    keep[0] = terms
    terms_out[...] = keep[0, pl.ds(me, 1), :]
    keep[1] = jnp.where((lane >= 104) & (lane < 112), names, corrected)
    fresh_out[...] = jnp.broadcast_to(keep[1, pl.ds(me, 1), :][None], fresh_out.shape)
    corrected_out[...] = corrected


def spread(line):
    diagonal = lane_of((16, LANES)) // CAP == row_of((16, LANES))
    x = jnp.where(diagonal, jnp.broadcast_to(line, (16, LANES)), 0.0)
    for shift in (64, 32, 16, 8):
        x = x + pltpu.roll(x, shift, 1)
    return x


def put(whole, active, step, line):
    columns = spread(line)
    star = lane_of((16, STARS))
    for s in range(CAP):
        whole = jnp.where(star == active[step, s], columns[:, s : s + 1], whole)
    return whole


def slot_terms(line):
    return jnp.transpose(spread(line))[0:CAP, 0:12]


def earlier_steps_kernel(me_of, *refs):
    state, active = refs[:2]
    corrected, terms = refs[2 : STEPS + 1], refs[STEPS + 1 : 2 * STEPS]
    state_out, terms_out = refs[2 * STEPS + 1 :]
    me = me_of()
    whole = state[...]
    for j in range(STEPS - 1):
        whole = put(whole, active, j, corrected[j][pl.ds(me, 1), :])
        terms_out[j] = slot_terms(terms[j][...])
    state_out[...] = whole


def last_kernel(me_of, *refs):
    gathered, target_rows, targets, state, earlier_terms, active = refs[:6]
    new_pos, new_vel, new_acc, new_jerk, terms_out, keep = refs[6:]
    me = me_of()
    corrected, terms, _ = correct_rows(STEPS - 1, gathered, target_rows, targets)
    keep[0] = terms
    keep[1] = corrected
    whole = put(state[...], active, STEPS - 1, keep[1, pl.ds(me, 1), :])
    terms_out[0 : STEPS - 1] = earlier_terms[...]
    terms_out[STEPS - 1] = slot_terms(keep[0, pl.ds(me, 1), :])
    for n, out in enumerate((new_pos, new_vel, new_acc, new_jerk)):
        out[...] = whole[3 * n : 3 * n + 3, :]


def struct(*shape):
    return jax.ShapeDtypeStruct(shape, jnp.float32)


def scratch(*shape):
    return pltpu.VMEM(shape, jnp.float32)


vmem = pl.BlockSpec(memory_space=pltpu.VMEM)
hbm = pl.BlockSpec(memory_space=pltpu.HBM)
smem = pl.BlockSpec(memory_space=pltpu.SMEM)
anywhere = pl.BlockSpec(memory_space=pl.ANY)


def call(kernel, operands, outs, work, specs=None, out_specs=None, flops=None):
    cost = None
    if flops:
        cost = pl.CostEstimate(flops=flops, bytes_accessed=1 << 20, transcendentals=0)
    return pl.pallas_call(
        kernel,
        out_shape=tuple(outs),
        in_specs=specs or [vmem] * len(operands),
        out_specs=out_specs or (vmem,) * len(outs),
        scratch_shapes=work,
        cost_estimate=cost,
        compiler_params=pltpu.CompilerParams(vmem_limit_bytes=8 << 20),
    )(*operands)


def send_all(x, axes):
    return lax.all_to_all(x, axes, split_axis=0, concat_axis=0, tiled=True)


def body(ncol, narrow, pos, vel, acc, jerk, masses, levels, active):
    masses, levels = masses.reshape(1, STARS), levels.reshape(1, STARS)
    pos, vel, acc, jerk, masses, levels, active = (
        pltpu.with_memory_space_constraint(a, pltpu.HBM)
        for a in (pos, vel, acc, jerk, masses, levels, active)
    )
    row_axes = ("core", "narrow")

    def me_of():
        return lax.axis_index("core") * narrow + lax.axis_index("narrow")

    block, rows, state = call(
        pack_kernel,
        (pos, vel, acc, jerk, masses, levels, active),
        (struct(ncol, 32, LANES), struct(NROW, 8, LANES), struct(16, STARS)),
        [scratch(3, STARS)] * 4
        + [scratch(1, STARS), pltpu.VMEM((1, STARS), jnp.int32)]
        + [scratch(32, LANES), scratch(8, LANES), pltpu.SemaphoreType.DMA((6,))],
        [hbm] * 6 + [smem],
    )
    target_rows = send_all(rows, row_axes).reshape(NROW * 8, LANES)
    block, target_rows = lax.optimization_barrier((block, target_rows))
    raw = send_all(block, "across").reshape(ncol * 32, LANES)

    sums_shape = struct(NROW, NROW // 2, LANES)
    source_shape = (7, 2 * ncol, LANES)
    slots = struct(NROW, LANES)
    splat_shape = (6 * TARGETS, LANES)
    list_shape = jax.ShapeDtypeStruct((STEPS, LIST), jnp.int32)
    list_work = [pltpu.SMEM(list_shape.shape, jnp.int32), pltpu.SemaphoreType.DMA]
    sum_work = list_work + [scratch(*source_shape), scratch(*splat_shape)]
    lists, splat = call(
        plan_kernel,
        (target_rows, target_rows),
        (list_shape, struct(*splat_shape)),
        [],
        [smem, vmem],
        (smem, vmem),
        flops=3 * 10**7,
    )
    (sums,) = call(
        functools.partial(first_force_kernel, ncol),
        (raw, lists, splat),
        (sums_shape,),
        sum_work,
        [vmem, anywhere, vmem],
    )
    corrected, terms = [], []
    targets = columns = None
    for step in range(STEPS):
        gathered = send_all(sums, row_axes)
        if step == STEPS - 1:
            break
        operands = [gathered, target_rows] + ([] if step == 0 else [targets])
        done, fresh, own_terms = call(
            functools.partial(correct_kernel, step, me_of),
            operands,
            (slots, struct(ncol, 1, LANES), struct(1, LANES)),
            [scratch(2, NROW, LANES)],
        )
        corrected.append(done)
        terms.append(own_terms)
        fresh = send_all(fresh, "across").reshape(ncol, LANES)
        operands = [raw, lists, target_rows, *corrected]
        static, splat, targets = call(
            functools.partial(static_kernel, step + 1, ncol),
            operands,
            (struct(8, LANES), struct(*splat_shape), slots),
            sum_work,
            [vmem, anywhere] + [vmem] * (step + 2),
            flops=3 * 10**7,
        )
        blocks = max(ncol // 16, 1) * (step + 1)
        operands = [static, splat, fresh] + ([] if step == 0 else [columns])
        outs, work = [sums_shape], [scratch(7, blocks, LANES)]
        if step + 1 < STEPS - 1:
            outs.append(struct(16 * blocks, LANES))
        else:
            work.insert(0, scratch(16 * blocks, LANES))
        sums, *columns = call(
            functools.partial(fresh_kernel, step + 1, ncol), operands, outs, work
        )
        if columns:
            (columns,) = columns
    state, earlier_terms = call(
        functools.partial(earlier_steps_kernel, me_of),
        (state, active, *corrected, *terms, sums),
        (struct(16, STARS), struct(STEPS - 1, CAP, 12)),
        [],
        [vmem, smem] + [vmem] * (2 * STEPS - 2) + [anywhere],
        flops=10**7,
    )
    *new, slot_rows = call(
        functools.partial(last_kernel, me_of),
        (gathered, target_rows, targets, state, earlier_terms, active),
        (struct(3, STARS),) * 4 + (struct(STEPS, CAP, 12),),
        [scratch(2, NROW, LANES)],
        [vmem] * 5 + [smem],
    )
    return (*new, jnp.swapaxes(slot_rows, 1, 2))


def solution(mesh):
    wide, narrow = mesh.shape["wide"], mesh.shape["narrow"]
    ncol = wide // 2
    every = ("across", "core", "narrow")
    finer = Mesh(mesh.devices.reshape(ncol, 2, narrow), every)
    in_specs = (P(None, every),) * 4 + (P(every), P(every), P(None, every))
    out_specs = (P(None, every),) * 4 + (P(None, None, every),)
    return jax.shard_map(
        functools.partial(body, ncol, narrow),
        mesh=finer,
        in_specs=in_specs,
        out_specs=out_specs,
        check_vma=False,
    )
```

time: 1660 us -> 149 us (0.09)
  waiting for transfers between devices: 1100 us -> 27.1 us
  blocking collectives: 451 us -> 54 us
  other arithmetic: 58.8 us -> 0 us
  local copies, waits for them, and re-layouts: 40.1 us -> 0 us
  Pallas kernels: 0 us -> 34 us
  starting transfers between devices: 0.16 us -> 32 us
    psum x4 -> x0, waiting for transfers between devices: 1100 us -> none  [body(): summed = lax.psum(partial_sums, ('wide', 'narrow'))]
    all_gather x4 -> x0, blocking collectives: 451 us -> none  [body(): targets = lax.all_gather(own_rows, ('wide', 'narrow'), axis=1, tiled=True)]
    all_to_all x0 -> x4, blocking collectives: none -> 54 us  [send_all(): return lax.all_to_all(x, axes, split_axis=0, concat_axis=0, tiled=True)]
    reduce_sum x64 -> x0, other arithmetic: 44.8 us -> none  [the longest x32 29.6 us: pair_sums(): accel_sum = jnp.sum(weight[None] * delta_x, -1)]
    pallas_call x0 -> x14, Pallas kernels: none -> 34 us  [call(): pl.pallas_call(kernel, out_shape=tuple(outs), in_specs=specs or [vmem] *...]
    all_to_all x0 -> x5, starting transfers between devices: none -> 32 us  [send_all(): return lax.all_to_all(x, axes, split_axis=0, concat_axis=0, tiled=True)]
    all_to_all x0 -> x5, waiting for transfers between devices: none -> 27.1 us  [send_all(): return lax.all_to_all(x, axes, split_axis=0, concat_axis=0, tiled=True)]
  transfers between devices with their start and end apart: 4 -> 5, of which waited for: 4 -> 5; matrix products, arithmetic and copies ran while one was open for 1% -> 0% of each run, Pallas kernels for 0% -> 13%
where the time goes in v3:
time: 149 us; the launch traced here: 148 us
  blocking collectives  54 us (36%)
  Pallas kernels  34 us (23%)
  starting transfers between devices  32 us (21%)
  waiting for transfers between devices  27.1 us (18%)
    all_to_all x4, blocking collectives, send_all(): return lax.all_to_all(x, axes, split_axis=0, concat_axis=0, tiled=True)  54 us
    pallas_call x14, Pallas kernels, call(): pl.pallas_call(kernel, out_shape=tuple(outs), in_specs=specs or [vmem] *...  34 us
    all_to_all x5, starting transfers between devices, send_all(): return lax.all_to_all(x, axes, split_axis=0, concat_axis=0, tiled=True)  32 us
    all_to_all x5, waiting for transfers between devices, send_all(): return lax.all_to_all(x, axes, split_axis=0, concat_axis=0, tiled=True)  27.1 us
  transfers between devices with their start and end apart: 5, of which 5 were waited for; matrix products, arithmetic and copies ran while one was open for 0% of the time, Pallas kernels for 13%

profile of v3, /device:TPU:1, one launch (start us, length us, event | category | flops | bytes accessed | tf_op | source)
XLA Modules:
  0.0 147.9 jit_solution(3439219597612440848)
XLA Ops:
  0.6 2.4 %shard_map.110 = (f32[32,32,128]{2,1,0:T(8,128)}, f32[16,8,128]{2,1,0:T(8,128)S(1)}, f32[16,256]{1,0:T(8,128)S(1)}) custom-call(f32[3,256]{1,0:T(4,128)} %refs_0_.1, f32[3,256]{1,0:T(4,128)} %refs_1_.2, f32[3,256]{1,0:T(4,128)} %refs_2_.1, f32[3,256]{1,0:T(4,128)} %refs_3_.1, f32[1,256]{1,0:T(1,128)} %bitcast.24, s32[1,256]{1,0:T(1,128)} %bitcast.25, ...), custom_call_target="tpu_custom_call" | custom-call | tf_op jit(solution)/shard_map/pallas_call | solution.py:419
  3.1 16.5 %all_to_all.45 = f32[16,8,128]{2,1,0:T(8,128)S(1)} all-to-all(f32[16,8,128]{2,1,0:T(8,128)S(1)} %get-tuple-element.42), channel_id=1, replica_groups=mesh['across'=32,'core'=2,'narrow'=8] {'core','narrow'}, dimensions={0} | all-to-all | bytes 131072 | tf_op jit(solution)/shard_map/all_to_all | solution.py:431
  19.6 12.0 %all-to-all-start.1 = ((f32[32,32,128]{2,1,0:T(8,128)}), f32[32,32,128]{2,1,0:T(8,128)S(1)}, u32[]{:S(2)}, u32[]{:S(2)}) async-start(f32[32,32,128]{2,1,0:T(8,128)} %get-tuple-element.43), calls=%async_computation.1 | async-start | bytes 1048576 | tf_op jit(solution)/shard_map/all_to_all | solution.py:431
  31.5 4.5 %shard_map.111 = (s32[4,160]{1,0:T(4,128)S(1)}, f32[768,128]{1,0:T(8,128)S(1)}) custom-call(f32[128,128]{1,0:T(8,128)S(1)} %bitcast.12, f32[128,128]{1,0:T(8,128)S(1)} %bitcast.13), custom_call_target="tpu_custom_call" | custom-call | flops 30000000 | bytes 1048576 | tf_op jit(solution)/shard_map/pallas_call | solution.py:419
  36.0 9.6 %all-to-all-done.1 = f32[32,32,128]{2,1,0:T(8,128)S(1)} async-done(((f32[32,32,128]{2,1,0:T(8,128)}), f32[32,32,128]{2,1,0:T(8,128)S(1)}, u32[]{:S(2)}, u32[]{:S(2)}) %all-to-all-start.1) | async-done | bytes 524320 | tf_op jit(solution)/shard_map/all_to_all | solution.py:431
  45.6 4.8 %shard_map.112 = f32[16,8,128]{2,1,0:T(8,128)S(1)} custom-call(f32[1024,128]{1,0:T(8,128)S(1)} %bitcast.8, s32[4,160]{1,0:T(4,128)S(1)} %get-tuple-element.45.lists_in.refs_1_, f32[768,128]{1,0:T(8,128)S(1)} %get-tuple-element.46.splat), custom_call_target="tpu_custom_call" | custom-call | tf_op jit(solution)/shard_map/pallas_call | solution.py:419
  50.4 13.6 %all_to_all.46.refs_0_ = f32[16,8,128]{2,1,0:T(8,128)S(1)} all-to-all(f32[16,8,128]{2,1,0:T(8,128)S(1)} %shard_map.112), channel_id=1, replica_groups=mesh['across'=32,'core'=2,'narrow'=8] {'core','narrow'}, dimensions={0} | all-to-all | bytes 131072 | tf_op jit(solution)/shard_map/all_to_all | solution.py:431
  64.1 0.9 shard_map.113
  64.9 5.5 %all-to-all-start.3 = ((f32[32,1,128]{2,1,0:T(1,128)}), f32[32,1,128]{2,1,0:T(1,128)S(1)}, u32[]{:S(2)}, u32[]{:S(2)}) async-start(f32[32,1,128]{2,1,0:T(1,128)} %get-tuple-element.50), calls=%async_computation.3 | async-start | bytes 32768 | tf_op jit(solution)/shard_map/all_to_all | solution.py:431
  70.5 4.5 %shard_map.114 = (f32[8,128]{1,0:T(8,128)S(1)}, f32[768,128]{1,0:T(8,128)S(1)}, f32[16,128]{1,0:T(8,128)S(1)}) custom-call(f32[1024,128]{1,0:T(8,128)S(1)} %bitcast.9, s32[4,160]{1,0:T(4,128)S(1)} %get-tuple-element.45.lists_in.refs_1_, f32[128,128]{1,0:T(8,128)S(1)} %bitcast.15, f32[16,128]{1,0:T(8,128)S(1)} %get-tuple-element.47.refs_3_.refs_2_), custom_call_target="tpu_custom_call" | custom-call | flops 30000000 | bytes 1048576 | tf_op jit(solution)/shard_map/pallas_call | solution.py:419
  75.0 4.0 %all-to-all-done.3 = f32[32,1,128]{2,1,0:T(1,128)S(1)} async-done(((f32[32,1,128]{2,1,0:T(1,128)}), f32[32,1,128]{2,1,0:T(1,128)S(1)}, u32[]{:S(2)}, u32[]{:S(2)}) %all-to-all-start.3) | async-done | bytes 16416 | tf_op jit(solution)/shard_map/all_to_all | solution.py:431
  79.0 0.4 shard_map.115
  79.5 11.9 %all_to_all.47.refs_0_ = f32[16,8,128]{2,1,0:T(8,128)S(1)} all-to-all(f32[16,8,128]{2,1,0:T(8,128)S(1)} %get-tuple-element.51), channel_id=1, replica_groups=mesh['across'=32,'core'=2,'narrow'=8] {'core','narrow'}, dimensions={0} | all-to-all | bytes 131072 | tf_op jit(solution)/shard_map/all_to_all | solution.py:431
  91.4 0.9 shard_map.116
  92.3 4.7 %all-to-all-start.5 = ((f32[32,1,128]{2,1,0:T(1,128)}), f32[32,1,128]{2,1,0:T(1,128)S(1)}, u32[]{:S(2)}, u32[]{:S(2)}) async-start(f32[32,1,128]{2,1,0:T(1,128)} %get-tuple-element.56), calls=%async_computation.5 | async-start | bytes 32768 | tf_op jit(solution)/shard_map/all_to_all | solution.py:431
  97.0 5.0 %shard_map.117 = (f32[8,128]{1,0:T(8,128)S(1)}, f32[768,128]{1,0:T(8,128)S(1)}, f32[16,128]{1,0:T(8,128)S(1)}) custom-call(f32[1024,128]{1,0:T(8,128)S(1)} %bitcast.10, s32[4,160]{1,0:T(4,128)S(1)} %get-tuple-element.45.lists_in.refs_1_, f32[128,128]{1,0:T(8,128)S(1)} %bitcast.17, f32[16,128]{1,0:T(8,128)S(1)} %get-tuple-element.47.refs_3_.refs_2_, ...), custom_call_target="tpu_custom_call" | custom-call | flops 30000000 | bytes 1048576 | tf_op jit(solution)/shard_map/pallas_call | solution.py:419
  102.0 3.6 %all-to-all-done.5 = f32[32,1,128]{2,1,0:T(1,128)S(1)} async-done(((f32[32,1,128]{2,1,0:T(1,128)}), f32[32,1,128]{2,1,0:T(1,128)S(1)}, u32[]{:S(2)}, u32[]{:S(2)}) %all-to-all-start.5) | async-done | bytes 16416 | tf_op jit(solution)/shard_map/all_to_all | solution.py:431
  105.6 0.6 shard_map.118
  106.2 11.9 %all_to_all.48.refs_0_ = f32[16,8,128]{2,1,0:T(8,128)S(1)} all-to-all(f32[16,8,128]{2,1,0:T(8,128)S(1)} %get-tuple-element.58), channel_id=1, replica_groups=mesh['across'=32,'core'=2,'narrow'=8] {'core','narrow'}, dimensions={0} | all-to-all | bytes 131072 | tf_op jit(solution)/shard_map/all_to_all | solution.py:431
  118.1 0.9 shard_map.119
  119.0 4.2 %all-to-all-start.7 = ((f32[32,1,128]{2,1,0:T(1,128)}), f32[32,1,128]{2,1,0:T(1,128)S(1)}, u32[]{:S(2)}, u32[]{:S(2)}) async-start(f32[32,1,128]{2,1,0:T(1,128)} %get-tuple-element.63), calls=%async_computation.7 | async-start | bytes 32768 | tf_op jit(solution)/shard_map/all_to_all | solution.py:431
  123.2 4.7 %shard_map.120 = (f32[8,128]{1,0:T(8,128)S(1)}, f32[768,128]{1,0:T(8,128)S(1)}, f32[16,128]{1,0:T(8,128)S(1)}) custom-call(f32[1024,128]{1,0:T(8,128)S(1)} %bitcast.11, s32[4,160]{1,0:T(4,128)S(1)} %get-tuple-element.45.lists_in.refs_1_, f32[128,128]{1,0:T(8,128)S(1)} %bitcast.19, f32[16,128]{1,0:T(8,128)S(1)} %get-tuple-element.47.refs_3_.refs_2_, ...), custom_call_target="tpu_custom_call" | custom-call | flops 30000000 | bytes 1048576 | tf_op jit(solution)/shard_map/pallas_call | solution.py:419
  127.9 3.9 %all-to-all-done.7 = f32[32,1,128]{2,1,0:T(1,128)S(1)} async-done(((f32[32,1,128]{2,1,0:T(1,128)}), f32[32,1,128]{2,1,0:T(1,128)S(1)}, u32[]{:S(2)}, u32[]{:S(2)}) %all-to-all-start.7) | async-done | bytes 16416 | tf_op jit(solution)/shard_map/all_to_all | solution.py:431
  131.7 1.5 shard_map.121.refs_8_
  133.2 5.6 %all-to-all-start.8 = ((f32[16,8,128]{2,1,0:T(8,128)}), f32[16,8,128]{2,1,0:T(8,128)S(1)}, u32[]{:S(2)}, u32[]{:S(2)}) async-start(f32[16,8,128]{2,1,0:T(8,128)} %shard_map.121.refs_8_), calls=%async_computation.8 | async-start | bytes 131072 | tf_op jit(solution)/shard_map/all_to_all | solution.py:431
  138.8 1.1 shard_map.122
  139.9 6.0 %all-to-all-done.8.refs_0_ = f32[16,8,128]{2,1,0:T(8,128)S(1)} async-done(((f32[16,8,128]{2,1,0:T(8,128)}), f32[16,8,128]{2,1,0:T(8,128)S(1)}, u32[]{:S(2)}, u32[]{:S(2)}) %all-to-all-start.8) | async-done | bytes 65568 | tf_op jit(solution)/shard_map/all_to_all | solution.py:431
  146.0 1.9 %shard_map.123 = (f32[3,256]{1,0:T(4,128)}, f32[3,256]{1,0:T(4,128)}, f32[3,256]{1,0:T(4,128)}, f32[3,256]{1,0:T(4,128)}, f32[4,8,12]{2,1,0:T(8,128)}) custom-call(f32[16,8,128]{2,1,0:T(8,128)S(1)} %all-to-all-done.8.refs_0_, f32[128,128]{1,0:T(8,128)S(1)} %bitcast.20, f32[16,128]{1,0:T(8,128)S(1)} %get-tuple-element.65.refs_2_, ...), custom_call_target="tpu_custom_call" | custom-call | tf_op jit(solution)/shard_map/pallas_call | solution.py:419
Async XLA Ops:
  19.6 26.0 %all-to-all-start.1 = ((f32[32,32,128]{2,1,0:T(8,128)}), f32[32,32,128]{2,1,0:T(8,128)S(1)}, u32[]{:S(2)}, u32[]{:S(2)}) async-start(f32[32,32,128]{2,1,0:T(8,128)} %get-tuple-element.43), calls=%async_computation.1 | async-start | bytes 1048576 | tf_op jit(solution)/shard_map/all_to_all | solution.py:431
  64.9 14.1 %all-to-all-start.3 = ((f32[32,1,128]{2,1,0:T(1,128)}), f32[32,1,128]{2,1,0:T(1,128)S(1)}, u32[]{:S(2)}, u32[]{:S(2)}) async-start(f32[32,1,128]{2,1,0:T(1,128)} %get-tuple-element.50), calls=%async_computation.3 | async-start | bytes 32768 | tf_op jit(solution)/shard_map/all_to_all | solution.py:431
  92.3 13.3 %all-to-all-start.5 = ((f32[32,1,128]{2,1,0:T(1,128)}), f32[32,1,128]{2,1,0:T(1,128)S(1)}, u32[]{:S(2)}, u32[]{:S(2)}) async-start(f32[32,1,128]{2,1,0:T(1,128)} %get-tuple-element.56), calls=%async_computation.5 | async-start | bytes 32768 | tf_op jit(solution)/shard_map/all_to_all | solution.py:431
  119.0 12.7 %all-to-all-start.7 = ((f32[32,1,128]{2,1,0:T(1,128)}), f32[32,1,128]{2,1,0:T(1,128)S(1)}, u32[]{:S(2)}, u32[]{:S(2)}) async-start(f32[32,1,128]{2,1,0:T(1,128)} %get-tuple-element.63), calls=%async_computation.7 | async-start | bytes 32768 | tf_op jit(solution)/shard_map/all_to_all | solution.py:431
  133.2 12.8 %all-to-all-start.8 = ((f32[16,8,128]{2,1,0:T(8,128)}), f32[16,8,128]{2,1,0:T(8,128)S(1)}, u32[]{:S(2)}, u32[]{:S(2)}) async-start(f32[16,8,128]{2,1,0:T(8,128)} %shard_map.121.refs_8_), calls=%async_computation.8 | async-start | bytes 131072 | tf_op jit(solution)/shard_map/all_to_all | solution.py:431

commit v4 on v3

--- a/solution.py
+++ b/solution.py
@@ -54,11 +54,11 @@
 
 
 def pack_kernel(*refs):
-    active, block_out, row_out, state, *held = refs[6:16]
-    block, rows, sems = refs[16:]
-    for copy in fetch(refs[:6], held, sems):
+    block_out, row_out, state, *held = refs[7:17]
+    block, rows, sems = refs[17:]
+    for copy in fetch(refs[:7], held, sems):
         copy.wait()
-    pos, vel, acc, jerk, mass, levels = held
+    pos, vel, acc, jerk, mass, levels, active = held
     for n, part in enumerate((pos, vel, acc, jerk)):
         state[3 * n : 3 * n + 3, :] = part[...]
     times = step_size * (1.0 - jnp.left_shift(1, levels[...]).astype(jnp.float32))
@@ -360,11 +360,11 @@
     return x
 
 
-def put(whole, active, step, line):
+def put(whole, names, line):
     columns = spread(line)
-    star = lane_of((16, STARS))
+    star = lane_of((16, STARS)).astype(jnp.float32)
     for s in range(CAP):
-        whole = jnp.where(star == active[step, s], columns[:, s : s + 1], whole)
+        whole = jnp.where(star == names[:, s : s + 1], columns[:, s : s + 1], whole)
     return whole
 
 
@@ -372,28 +372,21 @@
     return jnp.transpose(spread(line))[0:CAP, 0:12]
 
 
-def earlier_steps_kernel(me_of, *refs):
-    state, active = refs[:2]
-    corrected, terms = refs[2 : STEPS + 1], refs[STEPS + 1 : 2 * STEPS]
-    state_out, terms_out = refs[2 * STEPS + 1 :]
+def last_kernel(me_of, *refs):
+    gathered, target_rows, targets, state = refs[:4]
+    corrected, terms = refs[4 : STEPS + 3], refs[STEPS + 3 : 2 * STEPS + 2]
+    new_pos, new_vel, new_acc, new_jerk, terms_out, keep = refs[2 * STEPS + 2 :]
     me = me_of()
+    last_corrected, last_terms, _ = correct_rows(STEPS - 1, gathered, target_rows, targets)
+    keep[0] = last_terms
+    keep[1] = last_corrected
     whole = state[...]
-    for j in range(STEPS - 1):
-        whole = put(whole, active, j, corrected[j][pl.ds(me, 1), :])
-        terms_out[j] = slot_terms(terms[j][...])
-    state_out[...] = whole
-
-
-def last_kernel(me_of, *refs):
-    gathered, target_rows, targets, state, earlier_terms, active = refs[:6]
-    new_pos, new_vel, new_acc, new_jerk, terms_out, keep = refs[6:]
-    me = me_of()
-    corrected, terms, _ = correct_rows(STEPS - 1, gathered, target_rows, targets)
-    keep[0] = terms
-    keep[1] = corrected
-    whole = put(state[...], active, STEPS - 1, keep[1, pl.ds(me, 1), :])
-    terms_out[0 : STEPS - 1] = earlier_terms[...]
-    terms_out[STEPS - 1] = slot_terms(keep[0, pl.ds(me, 1), :])
+    for j in range(STEPS):
+        names = target_rows[pl.ds(CAP * me + STEPS + j, 1), :]
+        last = j == STEPS - 1
+        line = keep[1, pl.ds(me, 1), :] if last else corrected[j][pl.ds(me, 1), :]
+        whole = put(whole, names, line)
+        terms_out[j] = slot_terms(keep[0, pl.ds(me, 1), :] if last else terms[j][...])
     for n, out in enumerate((new_pos, new_vel, new_acc, new_jerk)):
         out[...] = whole[3 * n : 3 * n + 3, :]
 
@@ -448,8 +441,9 @@
         (struct(ncol, 32, LANES), struct(NROW, 8, LANES), struct(16, STARS)),
         [scratch(3, STARS)] * 4
         + [scratch(1, STARS), pltpu.VMEM((1, STARS), jnp.int32)]
-        + [scratch(32, LANES), scratch(8, LANES), pltpu.SemaphoreType.DMA((6,))],
-        [hbm] * 6 + [smem],
+        + [pltpu.SMEM((STEPS, CAP), jnp.int32)]
+        + [scratch(32, LANES), scratch(8, LANES), pltpu.SemaphoreType.DMA((7,))],
+        [hbm] * 7,
     )
     target_rows = send_all(rows, row_axes).reshape(NROW * 8, LANES)
     block, target_rows = lax.optimization_barrier((block, target_rows))
@@ -515,20 +509,11 @@
         )
         if columns:
             (columns,) = columns
-    state, earlier_terms = call(
-        functools.partial(earlier_steps_kernel, me_of),
-        (state, active, *corrected, *terms, sums),
-        (struct(16, STARS), struct(STEPS - 1, CAP, 12)),
-        [],
-        [vmem, smem] + [vmem] * (2 * STEPS - 2) + [anywhere],
-        flops=10**7,
-    )
     *new, slot_rows = call(
         functools.partial(last_kernel, me_of),
-        (gathered, target_rows, targets, state, earlier_terms, active),
+        (gathered, target_rows, targets, state, *corrected, *terms),
         (struct(3, STARS),) * 4 + (struct(STEPS, CAP, 12),),
         [scratch(2, NROW, LANES)],
-        [vmem] * 5 + [smem],
     )
     return (*new, jnp.swapaxes(slot_rows, 1, 2))
 

time: 149 us -> 147 us (0.987)
  blocking collectives: 54 us -> 65.9 us
  waiting for transfers between devices: 27.1 us -> 19.5 us
  starting transfers between devices: 32 us -> 27.6 us
    all_to_all x4 -> x5, blocking collectives: 54 us -> 65.9 us  [send_all(): return lax.all_to_all(x, axes, split_axis=0, concat_axis=0, tiled=True)]
    all_to_all x5 -> x4, waiting for transfers between devices: 27.1 us -> 19.5 us  [send_all(): return lax.all_to_all(x, axes, split_axis=0, concat_axis=0, tiled=True)]
    all_to_all x5 -> x4, starting transfers between devices: 32 us -> 27.6 us  [send_all(): return lax.all_to_all(x, axes, split_axis=0, concat_axis=0, tiled=True)]
    pallas_call x14 -> x13, Pallas kernels: 34 us -> 32.9 us  [call(): pl.pallas_call(kernel, out_shape=tuple(outs), in_specs=specs or [vmem] *...]
  transfers between devices with their start and end apart: 5 -> 4, of which waited for: 5 -> 4; matrix products, arithmetic and copies ran while one was open for 0% -> 0% of each run, Pallas kernels for 13% -> 14%
where the time goes in v4:
time: 147 us
  blocking collectives  65.9 us (45%)
  Pallas kernels  32.9 us (22%)
  starting transfers between devices  27.6 us (19%)
  waiting for transfers between devices  19.5 us (13%)
    all_to_all x5, blocking collectives, send_all(): return lax.all_to_all(x, axes, split_axis=0, concat_axis=0, tiled=True)  65.9 us
    pallas_call x13, Pallas kernels, call(): pl.pallas_call(kernel, out_shape=tuple(outs), in_specs=specs or [vmem] *...  32.9 us
    all_to_all x4, starting transfers between devices, send_all(): return lax.all_to_all(x, axes, split_axis=0, concat_axis=0, tiled=True)  27.6 us
    all_to_all x4, waiting for transfers between devices, send_all(): return lax.all_to_all(x, axes, split_axis=0, concat_axis=0, tiled=True)  19.5 us
  transfers between devices with their start and end apart: 4, of which 4 were waited for; matrix products, arithmetic and copies ran while one was open for 0% of the time, Pallas kernels for 14%

profile of v4, /device:TPU:1, one launch (start us, length us, event | category | flops | bytes accessed | tf_op | source)
XLA Modules:
  0.0 146.6 jit_solution(17643018128315406966)
XLA Ops:
  0.6 1.8 %shard_map.110 = (f32[32,32,128]{2,1,0:T(8,128)}, f32[16,8,128]{2,1,0:T(8,128)S(1)}, f32[16,256]{1,0:T(8,128)S(1)}) custom-call(f32[3,256]{1,0:T(4,128)} %refs_0_.1, f32[3,256]{1,0:T(4,128)} %refs_1_.1, f32[3,256]{1,0:T(4,128)} %refs_2_.1, f32[3,256]{1,0:T(4,128)} %refs_3_.1, f32[1,256]{1,0:T(1,128)} %bitcast.24, s32[1,256]{1,0:T(1,128)} %bitcast.25, ...), custom_call_target="tpu_custom_call" | custom-call | tf_op jit(solution)/shard_map/pallas_call | solution.py:412
  2.4 16.5 %all_to_all.45 = f32[16,8,128]{2,1,0:T(8,128)S(1)} all-to-all(f32[16,8,128]{2,1,0:T(8,128)S(1)} %get-tuple-element.40), channel_id=1, replica_groups=mesh['across'=32,'core'=2,'narrow'=8] {'core','narrow'}, dimensions={0} | all-to-all | bytes 131072 | tf_op jit(solution)/shard_map/all_to_all | solution.py:424
  18.9 12.0 %all-to-all-start.1 = ((f32[32,32,128]{2,1,0:T(8,128)}), f32[32,32,128]{2,1,0:T(8,128)S(1)}, u32[]{:S(2)}, u32[]{:S(2)}) async-start(f32[32,32,128]{2,1,0:T(8,128)} %get-tuple-element.41), calls=%async_computation.1 | async-start | bytes 1048576 | tf_op jit(solution)/shard_map/all_to_all | solution.py:424
  30.9 4.5 %shard_map.111 = (s32[4,160]{1,0:T(4,128)S(1)}, f32[768,128]{1,0:T(8,128)S(1)}) custom-call(f32[128,128]{1,0:T(8,128)S(1)} %bitcast.12, f32[128,128]{1,0:T(8,128)S(1)} %bitcast.13), custom_call_target="tpu_custom_call" | custom-call | flops 30000000 | bytes 1048576 | tf_op jit(solution)/shard_map/pallas_call | solution.py:412
  35.4 9.6 %all-to-all-done.1 = f32[32,32,128]{2,1,0:T(8,128)S(1)} async-done(((f32[32,32,128]{2,1,0:T(8,128)}), f32[32,32,128]{2,1,0:T(8,128)S(1)}, u32[]{:S(2)}, u32[]{:S(2)}) %all-to-all-start.1) | async-done | bytes 524320 | tf_op jit(solution)/shard_map/all_to_all | solution.py:424
  45.0 4.8 %shard_map.112 = f32[16,8,128]{2,1,0:T(8,128)S(1)} custom-call(f32[1024,128]{1,0:T(8,128)S(1)} %bitcast.8, s32[4,160]{1,0:T(4,128)S(1)} %get-tuple-element.43.lists_in.refs_1_, f32[768,128]{1,0:T(8,128)S(1)} %get-tuple-element.44.splat), custom_call_target="tpu_custom_call" | custom-call | tf_op jit(solution)/shard_map/pallas_call | solution.py:412
  49.8 13.6 %all_to_all.46.refs_0_ = f32[16,8,128]{2,1,0:T(8,128)S(1)} all-to-all(f32[16,8,128]{2,1,0:T(8,128)S(1)} %shard_map.112), channel_id=1, replica_groups=mesh['across'=32,'core'=2,'narrow'=8] {'core','narrow'}, dimensions={0} | all-to-all | bytes 131072 | tf_op jit(solution)/shard_map/all_to_all | solution.py:424
  63.4 0.9 shard_map.113
  64.3 5.3 %all-to-all-start.3 = ((f32[32,1,128]{2,1,0:T(1,128)}), f32[32,1,128]{2,1,0:T(1,128)S(1)}, u32[]{:S(2)}, u32[]{:S(2)}) async-start(f32[32,1,128]{2,1,0:T(1,128)} %get-tuple-element.48), calls=%async_computation.3 | async-start | bytes 32768 | tf_op jit(solution)/shard_map/all_to_all | solution.py:424
  69.6 5.3 %shard_map.114 = (f32[8,128]{1,0:T(8,128)S(1)}, f32[768,128]{1,0:T(8,128)S(1)}, f32[16,128]{1,0:T(8,128)S(1)}) custom-call(f32[1024,128]{1,0:T(8,128)S(1)} %bitcast.9, s32[4,160]{1,0:T(4,128)S(1)} %get-tuple-element.43.lists_in.refs_1_, f32[128,128]{1,0:T(8,128)S(1)} %bitcast.15, f32[16,128]{1,0:T(8,128)S(1)} %get-tuple-element.45.refs_3_.refs_4_), custom_call_target="tpu_custom_call" | custom-call | flops 30000000 | bytes 1048576 | tf_op jit(solution)/shard_map/pallas_call | solution.py:412
  74.9 3.2 %all-to-all-done.3 = f32[32,1,128]{2,1,0:T(1,128)S(1)} async-done(((f32[32,1,128]{2,1,0:T(1,128)}), f32[32,1,128]{2,1,0:T(1,128)S(1)}, u32[]{:S(2)}, u32[]{:S(2)}) %all-to-all-start.3) | async-done | bytes 16416 | tf_op jit(solution)/shard_map/all_to_all | solution.py:424
  78.1 0.4 shard_map.115
  78.6 11.9 %all_to_all.47.refs_0_ = f32[16,8,128]{2,1,0:T(8,128)S(1)} all-to-all(f32[16,8,128]{2,1,0:T(8,128)S(1)} %get-tuple-element.49), channel_id=1, replica_groups=mesh['across'=32,'core'=2,'narrow'=8] {'core','narrow'}, dimensions={0} | all-to-all | bytes 131072 | tf_op jit(solution)/shard_map/all_to_all | solution.py:424
  90.5 0.9 shard_map.116
  91.4 5.5 %all-to-all-start.5 = ((f32[32,1,128]{2,1,0:T(1,128)}), f32[32,1,128]{2,1,0:T(1,128)S(1)}, u32[]{:S(2)}, u32[]{:S(2)}) async-start(f32[32,1,128]{2,1,0:T(1,128)} %get-tuple-element.54), calls=%async_computation.5 | async-start | bytes 32768 | tf_op jit(solution)/shard_map/all_to_all | solution.py:424
  96.9 5.0 %shard_map.117 = (f32[8,128]{1,0:T(8,128)S(1)}, f32[768,128]{1,0:T(8,128)S(1)}, f32[16,128]{1,0:T(8,128)S(1)}) custom-call(f32[1024,128]{1,0:T(8,128)S(1)} %bitcast.10, s32[4,160]{1,0:T(4,128)S(1)} %get-tuple-element.43.lists_in.refs_1_, f32[128,128]{1,0:T(8,128)S(1)} %bitcast.17, f32[16,128]{1,0:T(8,128)S(1)} %get-tuple-element.45.refs_3_.refs_4_, ...), custom_call_target="tpu_custom_call" | custom-call | flops 30000000 | bytes 1048576 | tf_op jit(solution)/shard_map/pallas_call | solution.py:412
  101.9 3.6 %all-to-all-done.5 = f32[32,1,128]{2,1,0:T(1,128)S(1)} async-done(((f32[32,1,128]{2,1,0:T(1,128)}), f32[32,1,128]{2,1,0:T(1,128)S(1)}, u32[]{:S(2)}, u32[]{:S(2)}) %all-to-all-start.5) | async-done | bytes 16416 | tf_op jit(solution)/shard_map/all_to_all | solution.py:424
  105.5 0.6 shard_map.118
  106.1 11.9 %all_to_all.48.refs_0_ = f32[16,8,128]{2,1,0:T(8,128)S(1)} all-to-all(f32[16,8,128]{2,1,0:T(8,128)S(1)} %get-tuple-element.56), channel_id=1, replica_groups=mesh['across'=32,'core'=2,'narrow'=8] {'core','narrow'}, dimensions={0} | all-to-all | bytes 131072 | tf_op jit(solution)/shard_map/all_to_all | solution.py:424
  118.1 0.9 shard_map.119
  118.9 4.8 %all-to-all-start.7 = ((f32[32,1,128]{2,1,0:T(1,128)}), f32[32,1,128]{2,1,0:T(1,128)S(1)}, u32[]{:S(2)}, u32[]{:S(2)}) async-start(f32[32,1,128]{2,1,0:T(1,128)} %get-tuple-element.61), calls=%async_computation.7 | async-start | bytes 32768 | tf_op jit(solution)/shard_map/all_to_all | solution.py:424
  123.7 5.5 %shard_map.120 = (f32[8,128]{1,0:T(8,128)S(1)}, f32[768,128]{1,0:T(8,128)S(1)}, f32[16,128]{1,0:T(8,128)S(1)}) custom-call(f32[1024,128]{1,0:T(8,128)S(1)} %bitcast.11, s32[4,160]{1,0:T(4,128)S(1)} %get-tuple-element.43.lists_in.refs_1_, f32[128,128]{1,0:T(8,128)S(1)} %bitcast.19, f32[16,128]{1,0:T(8,128)S(1)} %get-tuple-element.45.refs_3_.refs_4_, ...), custom_call_target="tpu_custom_call" | custom-call | flops 30000000 | bytes 1048576 | tf_op jit(solution)/shard_map/pallas_call | solution.py:412
  129.2 3.1 %all-to-all-done.7 = f32[32,1,128]{2,1,0:T(1,128)S(1)} async-done(((f32[32,1,128]{2,1,0:T(1,128)}), f32[32,1,128]{2,1,0:T(1,128)S(1)}, u32[]{:S(2)}, u32[]{:S(2)}) %all-to-all-start.7) | async-done | bytes 16416 | tf_op jit(solution)/shard_map/all_to_all | solution.py:424
  132.3 0.8 shard_map.121
  133.1 11.9 %all_to_all.49.refs_0_ = f32[16,8,128]{2,1,0:T(8,128)S(1)} all-to-all(f32[16,8,128]{2,1,0:T(8,128)S(1)} %shard_map.121), channel_id=1, replica_groups=mesh['across'=32,'core'=2,'narrow'=8] {'core','narrow'}, dimensions={0} | all-to-all | bytes 131072 | tf_op jit(solution)/shard_map/all_to_all | solution.py:424
  145.0 1.5 %shard_map.122 = (f32[3,256]{1,0:T(4,128)}, f32[3,256]{1,0:T(4,128)}, f32[3,256]{1,0:T(4,128)}, f32[3,256]{1,0:T(4,128)}, f32[4,8,12]{2,1,0:T(8,128)}) custom-call(f32[16,8,128]{2,1,0:T(8,128)S(1)} %all_to_all.49.refs_0_, f32[128,128]{1,0:T(8,128)S(1)} %bitcast.20, f32[16,128]{1,0:T(8,128)S(1)} %get-tuple-element.63.refs_2_, ...), custom_call_target="tpu_custom_call" | custom-call | tf_op jit(solution)/shard_map/pallas_call | solution.py:412
Async XLA Ops:
  18.9 26.0 %all-to-all-start.1 = ((f32[32,32,128]{2,1,0:T(8,128)}), f32[32,32,128]{2,1,0:T(8,128)S(1)}, u32[]{:S(2)}, u32[]{:S(2)}) async-start(f32[32,32,128]{2,1,0:T(8,128)} %get-tuple-element.41), calls=%async_computation.1 | async-start | bytes 1048576 | tf_op jit(solution)/shard_map/all_to_all | solution.py:424
  64.3 13.8 %all-to-all-start.3 = ((f32[32,1,128]{2,1,0:T(1,128)}), f32[32,1,128]{2,1,0:T(1,128)S(1)}, u32[]{:S(2)}, u32[]{:S(2)}) async-start(f32[32,1,128]{2,1,0:T(1,128)} %get-tuple-element.48), calls=%async_computation.3 | async-start | bytes 32768 | tf_op jit(solution)/shard_map/all_to_all | solution.py:424
  91.4 14.1 %all-to-all-start.5 = ((f32[32,1,128]{2,1,0:T(1,128)}), f32[32,1,128]{2,1,0:T(1,128)S(1)}, u32[]{:S(2)}, u32[]{:S(2)}) async-start(f32[32,1,128]{2,1,0:T(1,128)} %get-tuple-element.54), calls=%async_computation.5 | async-start | bytes 32768 | tf_op jit(solution)/shard_map/all_to_all | solution.py:424
  118.9 13.4 %all-to-all-start.7 = ((f32[32,1,128]{2,1,0:T(1,128)}), f32[32,1,128]{2,1,0:T(1,128)S(1)}, u32[]{:S(2)}, u32[]{:S(2)}) async-start(f32[32,1,128]{2,1,0:T(1,128)} %get-tuple-element.61), calls=%async_computation.7 | async-start | bytes 32768 | tf_op jit(solution)/shard_map/all_to_all | solution.py:424

commit v5 on v4

--- a/solution.py
+++ b/solution.py
@@ -91,20 +91,29 @@
     row_out[...] = jnp.broadcast_to(rows[...][None], row_out.shape)
 
 
-def plan_kernel(scalars, target_rows, lists, splat):
-    for k in range(STEPS):
-
-        def peer(r, n):
+class Plan:
+    def __init__(self, target_rows, step, counts, scalars, sem, lists):
+        self.scalars, self.lists = scalars, lists
+        names = target_rows_at(target_rows, STEPS + step)
+        lane = lane_of((NROW, LANES))
+        named = jnp.where((names < float(STARS)) & (lane < CAP), 1.0, 0.0)
+        count = jnp.sum(named, axis=1, keepdims=True)
+        count = jnp.where(lane == row_of((NROW, LANES)), count, 0.0)
+        count = jnp.sum(count, axis=0, keepdims=True).astype(jnp.int32)
+        counts[...] = jnp.broadcast_to(count, (8, LANES))
+        self.copy = pltpu.make_async_copy(counts, scalars, sem)
+        self.copy.start()
+
+    def make(self):
+        self.copy.wait()
+        n = 0
+        for r in range(NROW):
             for s in range(CAP):
-                lists[k, n] = NROW * s + r
-                n = n + jnp.where(scalars[CAP * r + STEPS + k, s] < float(STARS), 1, 0)
-            return n
-
-        n = lax.fori_loop(0, NROW, peer, 0)
+                self.lists[n + s] = NROW * s + r
+            n = n + self.scalars[0, r]
         for u in range(AT_ONCE):
-            lists[k, n + u] = 0
-        lists[k, LIST - 1] = n
-    spread_targets(target_rows_at(target_rows, 0), splat, step_size)
+            self.lists[n + u] = 0
+        return n
 
 
 def predict_sources(raw, source, block_time, ncol):
@@ -138,40 +147,50 @@
     inverse = lax.rsqrt(radius_sq)
     inverse_sq = inverse * inverse
     weight = sources[6] * inverse * inverse_sq
-    closing = (dx * du + dy * dv + dz * dw) * (3.0 * inverse_sq)
+    closing = (dx * du + dy * dv + dz * dw) * inverse_sq
+    fx, fy, fz = weight * dx, weight * dy, weight * dz
     return (
-        sums[0] + weight * dx,
-        sums[1] + weight * dy,
-        sums[2] + weight * dz,
-        sums[3] + weight * (du - closing * dx),
-        sums[4] + weight * (dv - closing * dy),
-        sums[5] + weight * (dw - closing * dz),
+        sums[0] + fx,
+        sums[1] + fy,
+        sums[2] + fz,
+        sums[3] + weight * du,
+        sums[4] + weight * dv,
+        sums[5] + weight * dw,
+        sums[6] + closing * fx,
+        sums[7] + closing * fy,
+        sums[8] + closing * fz,
     )
+
+
+def force_and_jerk(sums):
+    return [*sums[:3], *(sums[n] - 3.0 * sums[n + 3] for n in range(3, 6))]
 
 
 def wide_row(ref, q, r):
     return jnp.broadcast_to(ref[q, pl.ds(r, 1), :], (8, LANES))
 
 
-def sum_listed(source, splat, part, lists, step):
+def sum_listed(source, splat, part, plan):
+    count = plan.make()
     chunks = source.shape[1] // 8
     part[...] = jnp.zeros(part.shape, jnp.float32)
     zero = jnp.zeros((8, LANES), jnp.float32)
 
     def some_targets(n, carry):
         for u in range(AT_ONCE):
-            i = lists[step, AT_ONCE * n + u]
+            i = plan.lists[AT_ONCE * n + u]
             target = [
                 jnp.broadcast_to(splat[pl.ds(q * TARGETS + i, 1), :], (8, LANES)) for q in range(6)
             ]
-            sums = (zero,) * 6
+            sums = (zero,) * 9
             for c in range(chunks):
                 sums = add_pairs(sums, [source[q, pl.ds(8 * c, 8), :] for q in range(7)], target)
+            sums = force_and_jerk(sums)
             for q in range(6):
                 part[pl.ds(q * TARGETS + i, 1), :] = jnp.sum(sums[q], axis=0, keepdims=True)
         return carry
 
-    lax.fori_loop(0, (lists[step, LIST - 1] + AT_ONCE - 1) // AT_ONCE, some_targets, 0)
+    lax.fori_loop(0, (count + AT_ONCE - 1) // AT_ONCE, some_targets, 0)
 
 
 def pack_sums(part):
@@ -188,14 +207,14 @@
     return [raw[pl.ds(16 * h + 15, ncol, stride=32), :] for h in range(2)]
 
 
-def first_force_kernel(ncol, raw, lists_in, splat, sums_out, lists, sem, source, part):
-    copy = pltpu.make_async_copy(lists_in, lists, sem)
-    copy.start()
+def first_force_kernel(ncol, raw, target_rows, sums_out, *work):
+    *plan_work, source, splat, part = work
+    plan = Plan(target_rows, 0, *plan_work)
     predict_sources(raw, source, step_size, ncol)
     for h, mass in enumerate(load_masses(raw, ncol)):
         source[6, pl.ds(h * ncol, ncol), :] = mass
-    copy.wait()
-    sum_listed(source, splat, part, lists, 0)
+    spread_targets(target_rows_at(target_rows, 0), splat, step_size)
+    sum_listed(source, splat, part, plan)
     sums_out[...] = jnp.broadcast_to(pack_sums(part)[None], sums_out.shape)
 
 
@@ -211,12 +230,11 @@
 
 
 def static_kernel(step, ncol, *refs):
-    raw, lists_in, target_rows = refs[:3]
-    corrected, refs = refs[3 : 3 + step], refs[3 + step :]
-    total_out, splat, targets, lists, sem, source, part = refs
+    raw, target_rows = refs[:2]
+    corrected, refs = refs[2 : 2 + step], refs[2 + step :]
+    total_out, splat, targets, *plan_work, source, part = refs
     block_time = (step + 1) * step_size
-    copy = pltpu.make_async_copy(lists_in, lists, sem)
-    copy.start()
+    plan = Plan(target_rows, step, *plan_work)
     rows = target_rows_at(target_rows, step)
     wanted = target_rows_at(target_rows, STEPS + step)
     for j in range(step):
@@ -234,8 +252,7 @@
             masses[h] = jnp.where(named == lane + float(h * LANES), 0.0, masses[h])
     for h in range(2):
         source[6, pl.ds(h * ncol, ncol), :] = masses[h]
-    copy.wait()
-    sum_listed(source, splat, part, lists, step)
+    sum_listed(source, splat, part, plan)
     total_out[...] = pack_sums(part)
 
 
@@ -288,13 +305,20 @@
     zero = jnp.zeros((8, LANES), jnp.float32)
     for g in range(GROUPS):
         target = [splat[pl.ds(q * TARGETS + 8 * g, 8), :] for q in range(6)]
-        sums = (zero,) * 6
+        sums = (zero,) * 9
         for b in range(blocks):
             sums = add_pairs(sums, [wide_row(source, q, b) for q in range(7)], target)
+        sums = force_and_jerk(sums)
         for q in range(6):
             line = jnp.sum(sums[q], axis=1, keepdims=True)
             total = jnp.where(lane == 64 * (g % 2) + CAP * q + g // 2, total + line, total)
-    sums_out[...] = jnp.broadcast_to(total[None], sums_out.shape)
+    if step == STEPS - 1:
+        upper = back(total, 64)
+        for r in range(CAP):
+            sums_out[r] = total[r : r + 1]
+            sums_out[CAP + r] = upper[r : r + 1]
+    else:
+        sums_out[...] = jnp.broadcast_to(total[None], sums_out.shape)
 
 
 def correct(old_acc, old_jerk, new_acc, new_jerk, interval):
@@ -307,15 +331,16 @@
     return (pos_step, vel_step)
 
 
-def correct_rows(step, gathered, target_rows, targets):
-    block_time = (step + 1) * step_size
+def add_peers(gathered):
     total = gathered[0]
     for p in range(1, NROW):
         total = total + gathered[p]
-    total = jnp.concatenate([total, back(total, 64)], axis=0)
-    z = target_rows_at(target_rows, 0) if step == 0 else targets[...]
-    names = target_rows_at(target_rows, STEPS + step)
-    lane = lane_of((NROW, LANES))
+    return jnp.concatenate([total, back(total, 64)], axis=0)
+
+
+def correct_rows(step, total, z, names):
+    block_time = (step + 1) * step_size
+    lane = lane_of(z.shape)
     tau = block_time - back(z, 96)
     old_acc, old_jerk = back(z, 48), back(z, 72)
     x, v = predict(z, back(z, 24), old_acc, old_jerk, tau)
@@ -333,7 +358,7 @@
     rest = jnp.where(lane < 120, block_time, z)
     corrected = lay(x + pos_step, v + vel_step, new_a, new_j, rest)
     terms = lay(new_a, new_j, pos_step, vel_step, jnp.zeros_like(z))
-    return jnp.where(filled, corrected, 0.0), jnp.where(filled, terms, 0.0), names
+    return jnp.where(filled, corrected, 0.0), jnp.where(filled, terms, 0.0)
 
 
 def correct_kernel(step, me_of, *refs):
@@ -343,7 +368,9 @@
         targets, *refs = refs
     corrected_out, fresh_out, terms_out, keep = refs
     me = me_of()
-    corrected, terms, names = correct_rows(step, gathered, target_rows, targets)
+    z = target_rows_at(target_rows, 0) if step == 0 else targets[...]
+    names = target_rows_at(target_rows, STEPS + step)
+    corrected, terms = correct_rows(step, add_peers(gathered), z, names)
     lane = lane_of((NROW, LANES))
     keep[0] = terms
     terms_out[...] = keep[0, pl.ds(me, 1), :]
@@ -375,18 +402,16 @@
 def last_kernel(me_of, *refs):
     gathered, target_rows, targets, state = refs[:4]
     corrected, terms = refs[4 : STEPS + 3], refs[STEPS + 3 : 2 * STEPS + 2]
-    new_pos, new_vel, new_acc, new_jerk, terms_out, keep = refs[2 * STEPS + 2 :]
+    new_pos, new_vel, new_acc, new_jerk, terms_out = refs[2 * STEPS + 2 :]
     me = me_of()
-    last_corrected, last_terms, _ = correct_rows(STEPS - 1, gathered, target_rows, targets)
-    keep[0] = last_terms
-    keep[1] = last_corrected
+    names = [target_rows[pl.ds(CAP * me + STEPS + j, 1), :] for j in range(STEPS)]
+    total = jnp.sum(gathered[...], axis=0, keepdims=True)
+    own, own_terms = correct_rows(STEPS - 1, total, targets[pl.ds(me, 1), :], names[-1])
     whole = state[...]
     for j in range(STEPS):
-        names = target_rows[pl.ds(CAP * me + STEPS + j, 1), :]
         last = j == STEPS - 1
-        line = keep[1, pl.ds(me, 1), :] if last else corrected[j][pl.ds(me, 1), :]
-        whole = put(whole, names, line)
-        terms_out[j] = slot_terms(keep[0, pl.ds(me, 1), :] if last else terms[j][...])
+        whole = put(whole, names[j], own if last else corrected[j][pl.ds(me, 1), :])
+        terms_out[j] = slot_terms(own_terms if last else terms[j][...])
     for n, out in enumerate((new_pos, new_vel, new_acc, new_jerk)):
         out[...] = whole[3 * n : 3 * n + 3, :]
 
@@ -453,24 +478,18 @@
     source_shape = (7, 2 * ncol, LANES)
     slots = struct(NROW, LANES)
     splat_shape = (6 * TARGETS, LANES)
-    list_shape = jax.ShapeDtypeStruct((STEPS, LIST), jnp.int32)
-    list_work = [pltpu.SMEM(list_shape.shape, jnp.int32), pltpu.SemaphoreType.DMA]
-    sum_work = list_work + [scratch(*source_shape), scratch(*splat_shape)]
-    lists, splat = call(
-        plan_kernel,
-        (target_rows, target_rows),
-        (list_shape, struct(*splat_shape)),
-        [],
-        [smem, vmem],
-        (smem, vmem),
-        flops=3 * 10**7,
-    )
+    plan_work = [
+        pltpu.VMEM((8, LANES), jnp.int32),
+        pltpu.SMEM((8, LANES), jnp.int32),
+        pltpu.SemaphoreType.DMA,
+        pltpu.SMEM((LIST,), jnp.int32),
+    ]
+    source_work, splat_work = scratch(*source_shape), scratch(*splat_shape)
     (sums,) = call(
         functools.partial(first_force_kernel, ncol),
-        (raw, lists, splat),
+        (raw, target_rows),
         (sums_shape,),
-        sum_work,
-        [vmem, anywhere, vmem],
+        [*plan_work, source_work, splat_work, splat_work],
     )
     corrected, terms = [], []
     targets = columns = None
@@ -488,13 +507,11 @@
         corrected.append(done)
         terms.append(own_terms)
         fresh = send_all(fresh, "across").reshape(ncol, LANES)
-        operands = [raw, lists, target_rows, *corrected]
         static, splat, targets = call(
             functools.partial(static_kernel, step + 1, ncol),
-            operands,
+            (raw, target_rows, *corrected),
             (struct(8, LANES), struct(*splat_shape), slots),
-            sum_work,
-            [vmem, anywhere] + [vmem] * (step + 2),
+            [*plan_work, source_work, splat_work],
             flops=3 * 10**7,
         )
         blocks = max(ncol // 16, 1) * (step + 1)
@@ -503,6 +520,7 @@
         if step + 1 < STEPS - 1:
             outs.append(struct(16 * blocks, LANES))
         else:
+            outs[0] = struct(NROW, 1, LANES)
             work.insert(0, scratch(16 * blocks, LANES))
         sums, *columns = call(
             functools.partial(fresh_kernel, step + 1, ncol), operands, outs, work
@@ -511,9 +529,9 @@
             (columns,) = columns
     *new, slot_rows = call(
         functools.partial(last_kernel, me_of),
-        (gathered, target_rows, targets, state, *corrected, *terms),
+        (gathered.reshape(NROW, LANES), target_rows, targets, state, *corrected, *terms),
         (struct(3, STARS),) * 4 + (struct(STEPS, CAP, 12),),
-        [scratch(2, NROW, LANES)],
+        [],
     )
     return (*new, jnp.swapaxes(slot_rows, 1, 2))
 

time: 147 us -> 146 us (level)
  blocking collectives: 65.9 us -> 91.5 us
  starting transfers between devices: 27.6 us -> 16.2 us
  waiting for transfers between devices: 19.5 us -> 9.63 us
  Pallas kernels: 32.9 us -> 27.1 us
    all_to_all x5 -> x6, blocking collectives: 65.9 us -> 91.5 us  [send_all(): return lax.all_to_all(x, axes, split_axis=0, concat_axis=0, tiled=True)]
    all_to_all x4 -> x3, starting transfers between devices: 27.6 us -> 16.2 us  [send_all(): return lax.all_to_all(x, axes, split_axis=0, concat_axis=0, tiled=True)]
    all_to_all x4 -> x3, waiting for transfers between devices: 19.5 us -> 9.63 us  [send_all(): return lax.all_to_all(x, axes, split_axis=0, concat_axis=0, tiled=True)]
    pallas_call x13 -> x12, Pallas kernels: 32.9 us -> 27.1 us  [call(): pl.pallas_call(kernel, out_shape=tuple(outs), in_specs=specs or [vmem] *...]
  transfers between devices with their start and end apart: 4 -> 3, of which waited for: 4 -> 3; matrix products, arithmetic and copies ran while one was open for 0% -> 0% of each run, Pallas kernels for 14% -> 11%
where the time goes in v5:
time: 146 us; the launch traced here: 145 us
  blocking collectives  91.5 us (63%)
  Pallas kernels  27.1 us (19%)
  starting transfers between devices  16.2 us (11%)
  waiting for transfers between devices  9.63 us (7%)
    all_to_all x6, blocking collectives, send_all(): return lax.all_to_all(x, axes, split_axis=0, concat_axis=0, tiled=True)  91.5 us
    pallas_call x12, Pallas kernels, call(): pl.pallas_call(kernel, out_shape=tuple(outs), in_specs=specs or [vmem] *...  27.1 us
    all_to_all x3, starting transfers between devices, send_all(): return lax.all_to_all(x, axes, split_axis=0, concat_axis=0, tiled=True)  16.2 us
    all_to_all x3, waiting for transfers between devices, send_all(): return lax.all_to_all(x, axes, split_axis=0, concat_axis=0, tiled=True)  9.63 us
  transfers between devices with their start and end apart: 3, of which 3 were waited for; matrix products, arithmetic and copies ran while one was open for 0% of the time, Pallas kernels for 11%

profile of v5, /device:TPU:1, one launch (start us, length us, event | category | flops | bytes accessed | tf_op | source)
XLA Modules:
  0.0 145.2 jit_solution(15914274944555816510)
XLA Ops:
  0.6 1.1 shard_map.110
  1.7 16.5 %all_to_all.45 = f32[16,8,128]{2,1,0:T(8,128)S(1)} all-to-all(f32[16,8,128]{2,1,0:T(8,128)S(1)} %get-tuple-element.38), channel_id=1, replica_groups=mesh['across'=32,'core'=2,'narrow'=8] {'core','narrow'}, dimensions={0} | all-to-all | bytes 131072 | tf_op jit(solution)/shard_map/all_to_all | solution.py:449
  18.2 25.8 %all_to_all.46 = f32[32,32,128]{2,1,0:T(8,128)S(1)} all-to-all(f32[32,32,128]{2,1,0:T(8,128)S(1)} %get-tuple-element.39), channel_id=1, replica_groups=mesh['across'=32,'core'=2,'narrow'=8] {'across'}, dimensions={0} | all-to-all | bytes 1048576 | tf_op jit(solution)/shard_map/all_to_all | solution.py:449
  44.0 4.2 %shard_map.111 = f32[16,8,128]{2,1,0:T(8,128)S(1)} custom-call(f32[1024,128]{1,0:T(8,128)S(1)} %bitcast.9, f32[128,128]{1,0:T(8,128)S(1)} %bitcast.13), custom_call_target="tpu_custom_call" | custom-call | tf_op jit(solution)/shard_map/pallas_call | solution.py:437
  48.2 13.6 %all_to_all.47.refs_0_ = f32[16,8,128]{2,1,0:T(8,128)S(1)} all-to-all(f32[16,8,128]{2,1,0:T(8,128)S(1)} %shard_map.111), channel_id=1, replica_groups=mesh['across'=32,'core'=2,'narrow'=8] {'core','narrow'}, dimensions={0} | all-to-all | bytes 131072 | tf_op jit(solution)/shard_map/all_to_all | solution.py:449
  61.9 0.9 shard_map.112
  62.7 5.7 %all-to-all-start.3 = ((f32[32,1,128]{2,1,0:T(1,128)}), f32[32,1,128]{2,1,0:T(1,128)S(1)}, u32[]{:S(2)}, u32[]{:S(2)}) async-start(f32[32,1,128]{2,1,0:T(1,128)} %get-tuple-element.44), calls=%async_computation.3 | async-start | bytes 32768 | tf_op jit(solution)/shard_map/all_to_all | solution.py:449
  68.4 5.4 %shard_map.113 = (f32[8,128]{1,0:T(8,128)S(1)}, f32[768,128]{1,0:T(8,128)S(1)}, f32[16,128]{1,0:T(8,128)S(1)}) custom-call(f32[1024,128]{1,0:T(8,128)S(1)} %bitcast.10, f32[128,128]{1,0:T(8,128)S(1)} %bitcast.15, f32[16,128]{1,0:T(8,128)S(1)} %get-tuple-element.41.refs_2_.refs_4_), custom_call_target="tpu_custom_call" | custom-call | flops 30000000 | bytes 1048576 | tf_op jit(solution)/shard_map/pallas_call | solution.py:437
  73.8 3.2 %all-to-all-done.3 = f32[32,1,128]{2,1,0:T(1,128)S(1)} async-done(((f32[32,1,128]{2,1,0:T(1,128)}), f32[32,1,128]{2,1,0:T(1,128)S(1)}, u32[]{:S(2)}, u32[]{:S(2)}) %all-to-all-start.3) | async-done | bytes 16416 | tf_op jit(solution)/shard_map/all_to_all | solution.py:449
  77.0 0.4 shard_map.114
  77.4 11.9 %all_to_all.48.refs_0_ = f32[16,8,128]{2,1,0:T(8,128)S(1)} all-to-all(f32[16,8,128]{2,1,0:T(8,128)S(1)} %get-tuple-element.45), channel_id=1, replica_groups=mesh['across'=32,'core'=2,'narrow'=8] {'core','narrow'}, dimensions={0} | all-to-all | bytes 131072 | tf_op jit(solution)/shard_map/all_to_all | solution.py:449
  89.4 0.9 shard_map.115
  90.3 5.2 %all-to-all-start.5 = ((f32[32,1,128]{2,1,0:T(1,128)}), f32[32,1,128]{2,1,0:T(1,128)S(1)}, u32[]{:S(2)}, u32[]{:S(2)}) async-start(f32[32,1,128]{2,1,0:T(1,128)} %get-tuple-element.50), calls=%async_computation.5 | async-start | bytes 32768 | tf_op jit(solution)/shard_map/all_to_all | solution.py:449
  95.5 5.1 %shard_map.116 = (f32[8,128]{1,0:T(8,128)S(1)}, f32[768,128]{1,0:T(8,128)S(1)}, f32[16,128]{1,0:T(8,128)S(1)}) custom-call(f32[1024,128]{1,0:T(8,128)S(1)} %bitcast.11, f32[128,128]{1,0:T(8,128)S(1)} %bitcast.17, f32[16,128]{1,0:T(8,128)S(1)} %get-tuple-element.41.refs_2_.refs_4_, f32[16,128]{1,0:T(8,128)S(1)} %get-tuple-element.47.refs_3_.refs_5_), custom_call_target="tpu_custom_call" | custom-call | flops 30000000 | bytes 1048576 | tf_op jit(solution)/shard_map/pallas_call | solution.py:437
  100.5 3.5 %all-to-all-done.5 = f32[32,1,128]{2,1,0:T(1,128)S(1)} async-done(((f32[32,1,128]{2,1,0:T(1,128)}), f32[32,1,128]{2,1,0:T(1,128)S(1)}, u32[]{:S(2)}, u32[]{:S(2)}) %all-to-all-start.5) | async-done | bytes 16416 | tf_op jit(solution)/shard_map/all_to_all | solution.py:449
  104.0 0.6 shard_map.117
  104.7 11.9 %all_to_all.49.refs_0_ = f32[16,8,128]{2,1,0:T(8,128)S(1)} all-to-all(f32[16,8,128]{2,1,0:T(8,128)S(1)} %get-tuple-element.52), channel_id=1, replica_groups=mesh['across'=32,'core'=2,'narrow'=8] {'core','narrow'}, dimensions={0} | all-to-all | bytes 131072 | tf_op jit(solution)/shard_map/all_to_all | solution.py:449
  116.6 0.9 shard_map.118
  117.5 5.3 %all-to-all-start.7 = ((f32[32,1,128]{2,1,0:T(1,128)}), f32[32,1,128]{2,1,0:T(1,128)S(1)}, u32[]{:S(2)}, u32[]{:S(2)}) async-start(f32[32,1,128]{2,1,0:T(1,128)} %get-tuple-element.57), calls=%async_computation.7 | async-start | bytes 32768 | tf_op jit(solution)/shard_map/all_to_all | solution.py:449
  122.7 5.6 %shard_map.119 = (f32[8,128]{1,0:T(8,128)S(1)}, f32[768,128]{1,0:T(8,128)S(1)}, f32[16,128]{1,0:T(8,128)S(1)}) custom-call(f32[1024,128]{1,0:T(8,128)S(1)} %bitcast.12, f32[128,128]{1,0:T(8,128)S(1)} %bitcast.19, f32[16,128]{1,0:T(8,128)S(1)} %get-tuple-element.41.refs_2_.refs_4_, f32[16,128]{1,0:T(8,128)S(1)} %get-tuple-element.47.refs_3_.refs_5_, ...), custom_call_target="tpu_custom_call" | custom-call | flops 30000000 | bytes 1048576 | tf_op jit(solution)/shard_map/pallas_call | solution.py:437
  128.3 3.0 %all-to-all-done.7 = f32[32,1,128]{2,1,0:T(1,128)S(1)} async-done(((f32[32,1,128]{2,1,0:T(1,128)}), f32[32,1,128]{2,1,0:T(1,128)S(1)}, u32[]{:S(2)}, u32[]{:S(2)}) %all-to-all-start.7) | async-done | bytes 16416 | tf_op jit(solution)/shard_map/all_to_all | solution.py:449
  131.3 0.9 shard_map.120
  132.2 11.7 %all_to_all.50 = f32[16,1,128]{2,1,0:T(1,128)S(1)} all-to-all(f32[16,1,128]{2,1,0:T(1,128)S(1)} %shard_map.120), channel_id=1, replica_groups=mesh['across'=32,'core'=2,'narrow'=8] {'core','narrow'}, dimensions={0} | all-to-all | bytes 16384 | tf_op jit(solution)/shard_map/all_to_all | solution.py:449
  143.8 1.3 shard_map.121
Async XLA Ops:
  62.7 14.3 %all-to-all-start.3 = ((f32[32,1,128]{2,1,0:T(1,128)}), f32[32,1,128]{2,1,0:T(1,128)S(1)}, u32[]{:S(2)}, u32[]{:S(2)}) async-start(f32[32,1,128]{2,1,0:T(1,128)} %get-tuple-element.44), calls=%async_computation.3 | async-start | bytes 32768 | tf_op jit(solution)/shard_map/all_to_all | solution.py:449
  90.3 13.8 %all-to-all-start.5 = ((f32[32,1,128]{2,1,0:T(1,128)}), f32[32,1,128]{2,1,0:T(1,128)S(1)}, u32[]{:S(2)}, u32[]{:S(2)}) async-start(f32[32,1,128]{2,1,0:T(1,128)} %get-tuple-element.50), calls=%async_computation.5 | async-start | bytes 32768 | tf_op jit(solution)/shard_map/all_to_all | solution.py:449
  117.5 13.8 %all-to-all-start.7 = ((f32[32,1,128]{2,1,0:T(1,128)}), f32[32,1,128]{2,1,0:T(1,128)S(1)}, u32[]{:S(2)}, u32[]{:S(2)}) async-start(f32[32,1,128]{2,1,0:T(1,128)} %get-tuple-element.57), calls=%async_computation.7 | async-start | bytes 32768 | tf_op jit(solution)/shard_map/all_to_all | solution.py:449

commit v6 on v5

--- a/solution.py
+++ b/solution.py
@@ -1,4 +1,5 @@
 import functools
+import math
 
 import jax
 import jax.numpy as jnp
@@ -449,16 +450,19 @@
     return lax.all_to_all(x, axes, split_axis=0, concat_axis=0, tiled=True)
 
 
-def body(ncol, narrow, pos, vel, acc, jerk, masses, levels, active):
+def body(sizes, row_axes, col_axes, pos, vel, acc, jerk, masses, levels, active):
     masses, levels = masses.reshape(1, STARS), levels.reshape(1, STARS)
     pos, vel, acc, jerk, masses, levels, active = (
         pltpu.with_memory_space_constraint(a, pltpu.HBM)
         for a in (pos, vel, acc, jerk, masses, levels, active)
     )
-    row_axes = ("core", "narrow")
+    ncol = math.prod(sizes[axis] for axis in col_axes)
 
     def me_of():
-        return lax.axis_index("core") * narrow + lax.axis_index("narrow")
+        me = 0
+        for axis in row_axes:
+            me = me * sizes[axis] + lax.axis_index(axis)
+        return me
 
     block, rows, state = call(
         pack_kernel,
@@ -472,7 +476,7 @@
     )
     target_rows = send_all(rows, row_axes).reshape(NROW * 8, LANES)
     block, target_rows = lax.optimization_barrier((block, target_rows))
-    raw = send_all(block, "across").reshape(ncol * 32, LANES)
+    raw = send_all(block, col_axes).reshape(ncol * 32, LANES)
 
     sums_shape = struct(NROW, NROW // 2, LANES)
     source_shape = (7, 2 * ncol, LANES)
@@ -506,7 +510,7 @@
         )
         corrected.append(done)
         terms.append(own_terms)
-        fresh = send_all(fresh, "across").reshape(ncol, LANES)
+        fresh = send_all(fresh, col_axes).reshape(ncol, LANES)
         static, splat, targets = call(
             functools.partial(static_kernel, step + 1, ncol),
             (raw, target_rows, *corrected),
@@ -537,14 +541,14 @@
 
 
 def solution(mesh):
-    wide, narrow = mesh.shape["wide"], mesh.shape["narrow"]
-    ncol = wide // 2
-    every = ("across", "core", "narrow")
-    finer = Mesh(mesh.devices.reshape(ncol, 2, narrow), every)
+    sizes = {"x": 4, "z": mesh.shape["wide"] // 8, "core": 2, "narrow": mesh.shape["narrow"]}
+    row_axes, col_axes = ("core", "narrow"), ("z", "x")
+    every = tuple(sizes)
+    finer = Mesh(mesh.devices.reshape(tuple(sizes.values())), every)
     in_specs = (P(None, every),) * 4 + (P(every), P(every), P(None, every))
     out_specs = (P(None, every),) * 4 + (P(None, None, every),)
     return jax.shard_map(
-        functools.partial(body, ncol, narrow),
+        functools.partial(body, sizes, row_axes, col_axes),
         mesh=finer,
         in_specs=in_specs,
         out_specs=out_specs,

time: 146 us -> 144 us (0.986)
  starting transfers between devices: 16.2 us -> 13 us
    all_to_all x3, starting transfers between devices: 16.2 us -> 13 us  [send_all(): return lax.all_to_all(x, axes, split_axis=0, concat_axis=0, tiled=True)]
  transfers between devices with their start and end apart: 3 -> 3, of which waited for: 3 -> 3; matrix products, arithmetic and copies ran while one was open for 0% -> 0% of each run, Pallas kernels for 11% -> 10%
where the time goes in v6:
time: 144 us; the launch traced here: 143 us
  blocking collectives  92.2 us (64%)
  Pallas kernels  26.8 us (19%)
  starting transfers between devices  13 us (9%)
  waiting for transfers between devices  10.7 us (7%)
    all_to_all x6, blocking collectives, send_all(): return lax.all_to_all(x, axes, split_axis=0, concat_axis=0, tiled=True)  92.2 us
    pallas_call x12, Pallas kernels, call(): pl.pallas_call(kernel, out_shape=tuple(outs), in_specs=specs or [vmem] *...  26.8 us
    all_to_all x3, starting transfers between devices, send_all(): return lax.all_to_all(x, axes, split_axis=0, concat_axis=0, tiled=True)  13 us
    all_to_all x3, waiting for transfers between devices, send_all(): return lax.all_to_all(x, axes, split_axis=0, concat_axis=0, tiled=True)  10.7 us
  transfers between devices with their start and end apart: 3, of which 3 were waited for; matrix products, arithmetic and copies ran while one was open for 0% of the time, Pallas kernels for 10%

profile of v6, /device:TPU:1, one launch (start us, length us, event | category | flops | bytes accessed | tf_op | source)
XLA Modules:
  0.0 143.3 jit_solution(14565228722697416777)
XLA Ops:
  0.6 1.1 shard_map.110
  1.7 16.5 %all_to_all.45 = f32[16,8,128]{2,1,0:T(8,128)S(1)} all-to-all(f32[16,8,128]{2,1,0:T(8,128)S(1)} %get-tuple-element.38), channel_id=1, replica_groups=mesh['x'=4,'z'=8,'core'=2,'narrow'=8] {'core','narrow'}, dimensions={0} | all-to-all | bytes 131072 | tf_op jit(solution)/shard_map/all_to_all | solution.py:450
  18.2 27.2 %all_to_all.46 = f32[32,32,128]{2,1,0:T(8,128)S(1)} all-to-all(f32[32,32,128]{2,1,0:T(8,128)S(1)} %get-tuple-element.39), channel_id=1, replica_groups=mesh['x'=4,'z'=8,'core'=2,'narrow'=8] {'z','x'}, dimensions={0} | all-to-all | bytes 1048576 | tf_op jit(solution)/shard_map/all_to_all | solution.py:450
  45.4 5.0 %shard_map.111 = f32[16,8,128]{2,1,0:T(8,128)S(1)} custom-call(f32[1024,128]{1,0:T(8,128)S(1)} %bitcast.9, f32[128,128]{1,0:T(8,128)S(1)} %bitcast.13), custom_call_target="tpu_custom_call" | custom-call | tf_op jit(solution)/shard_map/pallas_call | solution.py:438
  50.4 13.0 %all_to_all.47.refs_0_ = f32[16,8,128]{2,1,0:T(8,128)S(1)} all-to-all(f32[16,8,128]{2,1,0:T(8,128)S(1)} %shard_map.111), channel_id=1, replica_groups=mesh['x'=4,'z'=8,'core'=2,'narrow'=8] {'core','narrow'}, dimensions={0} | all-to-all | bytes 131072 | tf_op jit(solution)/shard_map/all_to_all | solution.py:450
  63.4 0.9 shard_map.112
  64.3 3.9 %all-to-all-start.3 = ((f32[32,1,128]{2,1,0:T(1,128)}), f32[32,1,128]{2,1,0:T(1,128)S(1)}, u32[]{:S(2)}, u32[]{:S(2)}) async-start(f32[32,1,128]{2,1,0:T(1,128)} %get-tuple-element.44), calls=%async_computation.3 | async-start | bytes 32768 | tf_op jit(solution)/shard_map/all_to_all | solution.py:450
  68.2 5.8 %shard_map.113 = (f32[8,128]{1,0:T(8,128)S(1)}, f32[768,128]{1,0:T(8,128)S(1)}, f32[16,128]{1,0:T(8,128)S(1)}) custom-call(f32[1024,128]{1,0:T(8,128)S(1)} %bitcast.10, f32[128,128]{1,0:T(8,128)S(1)} %bitcast.15, f32[16,128]{1,0:T(8,128)S(1)} %get-tuple-element.41.refs_2_.refs_4_), custom_call_target="tpu_custom_call" | custom-call | flops 30000000 | bytes 1048576 | tf_op jit(solution)/shard_map/pallas_call | solution.py:438
  74.0 2.7 %all-to-all-done.3 = f32[32,1,128]{2,1,0:T(1,128)S(1)} async-done(((f32[32,1,128]{2,1,0:T(1,128)}), f32[32,1,128]{2,1,0:T(1,128)S(1)}, u32[]{:S(2)}, u32[]{:S(2)}) %all-to-all-start.3) | async-done | bytes 16416 | tf_op jit(solution)/shard_map/all_to_all | solution.py:450
  76.7 0.4 shard_map.114
  77.1 11.9 %all_to_all.48.refs_0_ = f32[16,8,128]{2,1,0:T(8,128)S(1)} all-to-all(f32[16,8,128]{2,1,0:T(8,128)S(1)} %get-tuple-element.45), channel_id=1, replica_groups=mesh['x'=4,'z'=8,'core'=2,'narrow'=8] {'core','narrow'}, dimensions={0} | all-to-all | bytes 131072 | tf_op jit(solution)/shard_map/all_to_all | solution.py:450
  89.1 0.9 shard_map.115
  89.9 4.5 %all-to-all-start.5 = ((f32[32,1,128]{2,1,0:T(1,128)}), f32[32,1,128]{2,1,0:T(1,128)S(1)}, u32[]{:S(2)}, u32[]{:S(2)}) async-start(f32[32,1,128]{2,1,0:T(1,128)} %get-tuple-element.50), calls=%async_computation.5 | async-start | bytes 32768 | tf_op jit(solution)/shard_map/all_to_all | solution.py:450
  94.4 4.3 %shard_map.116 = (f32[8,128]{1,0:T(8,128)S(1)}, f32[768,128]{1,0:T(8,128)S(1)}, f32[16,128]{1,0:T(8,128)S(1)}) custom-call(f32[1024,128]{1,0:T(8,128)S(1)} %bitcast.11, f32[128,128]{1,0:T(8,128)S(1)} %bitcast.17, f32[16,128]{1,0:T(8,128)S(1)} %get-tuple-element.41.refs_2_.refs_4_, f32[16,128]{1,0:T(8,128)S(1)} %get-tuple-element.47.refs_3_.refs_5_), custom_call_target="tpu_custom_call" | custom-call | flops 30000000 | bytes 1048576 | tf_op jit(solution)/shard_map/pallas_call | solution.py:438
  98.7 4.2 %all-to-all-done.5 = f32[32,1,128]{2,1,0:T(1,128)S(1)} async-done(((f32[32,1,128]{2,1,0:T(1,128)}), f32[32,1,128]{2,1,0:T(1,128)S(1)}, u32[]{:S(2)}, u32[]{:S(2)}) %all-to-all-start.5) | async-done | bytes 16416 | tf_op jit(solution)/shard_map/all_to_all | solution.py:450
  102.9 0.6 shard_map.117
  103.6 11.9 %all_to_all.49.refs_0_ = f32[16,8,128]{2,1,0:T(8,128)S(1)} all-to-all(f32[16,8,128]{2,1,0:T(8,128)S(1)} %get-tuple-element.52), channel_id=1, replica_groups=mesh['x'=4,'z'=8,'core'=2,'narrow'=8] {'core','narrow'}, dimensions={0} | all-to-all | bytes 131072 | tf_op jit(solution)/shard_map/all_to_all | solution.py:450
  115.5 0.9 shard_map.118
  116.3 4.6 %all-to-all-start.7 = ((f32[32,1,128]{2,1,0:T(1,128)}), f32[32,1,128]{2,1,0:T(1,128)S(1)}, u32[]{:S(2)}, u32[]{:S(2)}) async-start(f32[32,1,128]{2,1,0:T(1,128)} %get-tuple-element.57), calls=%async_computation.7 | async-start | bytes 32768 | tf_op jit(solution)/shard_map/all_to_all | solution.py:450
  121.0 4.8 %shard_map.119 = (f32[8,128]{1,0:T(8,128)S(1)}, f32[768,128]{1,0:T(8,128)S(1)}, f32[16,128]{1,0:T(8,128)S(1)}) custom-call(f32[1024,128]{1,0:T(8,128)S(1)} %bitcast.12, f32[128,128]{1,0:T(8,128)S(1)} %bitcast.19, f32[16,128]{1,0:T(8,128)S(1)} %get-tuple-element.41.refs_2_.refs_4_, f32[16,128]{1,0:T(8,128)S(1)} %get-tuple-element.47.refs_3_.refs_5_, ...), custom_call_target="tpu_custom_call" | custom-call | flops 30000000 | bytes 1048576 | tf_op jit(solution)/shard_map/pallas_call | solution.py:438
  125.8 3.7 %all-to-all-done.7 = f32[32,1,128]{2,1,0:T(1,128)S(1)} async-done(((f32[32,1,128]{2,1,0:T(1,128)}), f32[32,1,128]{2,1,0:T(1,128)S(1)}, u32[]{:S(2)}, u32[]{:S(2)}) %all-to-all-start.7) | async-done | bytes 16416 | tf_op jit(solution)/shard_map/all_to_all | solution.py:450
  129.5 0.9 shard_map.120
  130.4 11.7 %all_to_all.50 = f32[16,1,128]{2,1,0:T(1,128)S(1)} all-to-all(f32[16,1,128]{2,1,0:T(1,128)S(1)} %shard_map.120), channel_id=1, replica_groups=mesh['x'=4,'z'=8,'core'=2,'narrow'=8] {'core','narrow'}, dimensions={0} | all-to-all | bytes 16384 | tf_op jit(solution)/shard_map/all_to_all | solution.py:450
  142.0 1.3 shard_map.121
Async XLA Ops:
  64.3 12.4 %all-to-all-start.3 = ((f32[32,1,128]{2,1,0:T(1,128)}), f32[32,1,128]{2,1,0:T(1,128)S(1)}, u32[]{:S(2)}, u32[]{:S(2)}) async-start(f32[32,1,128]{2,1,0:T(1,128)} %get-tuple-element.44), calls=%async_computation.3 | async-start | bytes 32768 | tf_op jit(solution)/shard_map/all_to_all | solution.py:450
  89.9 13.0 %all-to-all-start.5 = ((f32[32,1,128]{2,1,0:T(1,128)}), f32[32,1,128]{2,1,0:T(1,128)S(1)}, u32[]{:S(2)}, u32[]{:S(2)}) async-start(f32[32,1,128]{2,1,0:T(1,128)} %get-tuple-element.50), calls=%async_computation.5 | async-start | bytes 32768 | tf_op jit(solution)/shard_map/all_to_all | solution.py:450
  116.3 13.1 %all-to-all-start.7 = ((f32[32,1,128]{2,1,0:T(1,128)}), f32[32,1,128]{2,1,0:T(1,128)S(1)}, u32[]{:S(2)}, u32[]{:S(2)}) async-start(f32[32,1,128]{2,1,0:T(1,128)} %get-tuple-element.57), calls=%async_computation.7 | async-start | bytes 32768 | tf_op jit(solution)/shard_map/all_to_all | solution.py:450

commit v7 on v6

--- a/solution.py
+++ b/solution.py
@@ -18,6 +18,7 @@
 NROW = 16
 TARGETS = NROW * CAP
 GROUPS = TARGETS // 8
+BLOCK = 29
 AT_ONCE = 8
 LIST = TARGETS + 32
 
@@ -71,10 +72,13 @@
     for k in range(STEPS):
         for s in range(CAP):
             names = jnp.where(lane == CAP * k + s, active[k, s], names)
-    block[0:16, :] = whole[:, :LANES]
-    block[16:32, :] = whole[:, LANES:]
-    block[13:14, :] = names.astype(jnp.float32)
-    block_out[...] = jnp.broadcast_to(block[...][None], block_out.shape)
+    for h in range(2):
+        block[14 * h : 14 * h + 13, :] = whole[0:13, LANES * h : LANES * h + LANES]
+        block[14 * h + 13 : 14 * h + 14, :] = whole[15:16, LANES * h : LANES * h + LANES]
+    block[28:29, :] = names.astype(jnp.float32)
+    filled = block[0:BLOCK, :]
+    for p in range(block_out.shape[0] // BLOCK):
+        block_out[BLOCK * p : BLOCK * p + BLOCK, :] = filled
     lane = lane_of((16, LANES))
     diagonal = lane // CAP == row_of((16, LANES))
     slot = lane % CAP
@@ -122,7 +126,7 @@
         at = pl.ds(h * ncol, ncol)
 
         def load(q):
-            return raw[pl.ds(16 * h + q, ncol, stride=32), :]
+            return raw[pl.ds(14 * h + q, ncol, stride=BLOCK), :]
 
         tau = block_time - load(12)
         for c in range(3):
@@ -205,7 +209,7 @@
 
 
 def load_masses(raw, ncol):
-    return [raw[pl.ds(16 * h + 15, ncol, stride=32), :] for h in range(2)]
+    return [raw[pl.ds(14 * h + 13, ncol, stride=BLOCK), :] for h in range(2)]
 
 
 def first_force_kernel(ncol, raw, target_rows, sums_out, *work):
@@ -245,7 +249,7 @@
     spread_targets(rows, splat, block_time)
     predict_sources(raw, source, block_time, ncol)
     masses = load_masses(raw, ncol)
-    names = raw[pl.ds(13, ncol, stride=32), :]
+    names = raw[pl.ds(28, ncol, stride=BLOCK), :]
     lane = lane_of((ncol, LANES)).astype(jnp.float32)
     for at in range(CAP * step):
         named = jnp.broadcast_to(names[:, at : at + 1], (ncol, LANES))
@@ -467,7 +471,7 @@
     block, rows, state = call(
         pack_kernel,
         (pos, vel, acc, jerk, masses, levels, active),
-        (struct(ncol, 32, LANES), struct(NROW, 8, LANES), struct(16, STARS)),
+        (struct(ncol * BLOCK, LANES), struct(NROW, 8, LANES), struct(16, STARS)),
         [scratch(3, STARS)] * 4
         + [scratch(1, STARS), pltpu.VMEM((1, STARS), jnp.int32)]
         + [pltpu.SMEM((STEPS, CAP), jnp.int32)]
@@ -476,7 +480,8 @@
     )
     target_rows = send_all(rows, row_axes).reshape(NROW * 8, LANES)
     block, target_rows = lax.optimization_barrier((block, target_rows))
-    raw = send_all(block, col_axes).reshape(ncol * 32, LANES)
+    block = block.reshape(ncol, 1, BLOCK * LANES)
+    raw = send_all(block, col_axes).reshape(ncol * BLOCK, LANES)
 
     sums_shape = struct(NROW, NROW // 2, LANES)
     source_shape = (7, 2 * ncol, LANES)

time: 144 us -> 143 us (level)
  no operation moved by 1% of the time
where the time goes in v7:
time: 143 us
  blocking collectives  91 us (64%)
  Pallas kernels  26.1 us (18%)
  starting transfers between devices  13 us (9%)
  waiting for transfers between devices  11.7 us (8%)
    all_to_all x6, blocking collectives, send_all(): return lax.all_to_all(x, axes, split_axis=0, concat_axis=0, tiled=True)  91 us
    pallas_call x12, Pallas kernels, call(): pl.pallas_call(kernel, out_shape=tuple(outs), in_specs=specs or [vmem] *...  26.1 us
    all_to_all x3, starting transfers between devices, send_all(): return lax.all_to_all(x, axes, split_axis=0, concat_axis=0, tiled=True)  13 us
    all_to_all x3, waiting for transfers between devices, send_all(): return lax.all_to_all(x, axes, split_axis=0, concat_axis=0, tiled=True)  11.7 us
  transfers between devices with their start and end apart: 3, of which 3 were waited for; matrix products, arithmetic and copies ran while one was open for 0% of the time, Pallas kernels for 10%

profile of v7, /device:TPU:1, one launch (start us, length us, event | category | flops | bytes accessed | tf_op | source)
XLA Modules:
  0.0 142.5 jit_solution(17843400039075889883)
XLA Ops:
  0.6 1.1 shard_map.110
  1.7 16.5 %all_to_all.45 = f32[16,8,128]{2,1,0:T(8,128)S(1)} all-to-all(f32[16,8,128]{2,1,0:T(8,128)S(1)} %get-tuple-element.38), channel_id=1, replica_groups=mesh['x'=4,'z'=8,'core'=2,'narrow'=8] {'core','narrow'}, dimensions={0} | all-to-all | bytes 131072 | tf_op jit(solution)/shard_map/all_to_all | solution.py:454
  18.2 26.3 %all_to_all.46 = f32[32,1,3712]{2,1,0:T(1,128)S(1)} all-to-all(f32[32,1,3712]{2,1,0:T(1,128)S(1)} %bitcast.22), channel_id=1, replica_groups=mesh['x'=4,'z'=8,'core'=2,'narrow'=8] {'z','x'}, dimensions={0} | all-to-all | bytes 950272 | tf_op jit(solution)/shard_map/all_to_all | solution.py:454
  44.5 5.4 %shard_map.111 = f32[16,8,128]{2,1,0:T(8,128)S(1)} custom-call(f32[928,128]{1,0:T(8,128)S(1)} %bitcast.10, f32[128,128]{1,0:T(8,128)S(1)} %bitcast.14), custom_call_target="tpu_custom_call" | custom-call | tf_op jit(solution)/shard_map/pallas_call | solution.py:442
  49.9 12.9 %all_to_all.47.refs_0_ = f32[16,8,128]{2,1,0:T(8,128)S(1)} all-to-all(f32[16,8,128]{2,1,0:T(8,128)S(1)} %shard_map.111), channel_id=1, replica_groups=mesh['x'=4,'z'=8,'core'=2,'narrow'=8] {'core','narrow'}, dimensions={0} | all-to-all | bytes 131072 | tf_op jit(solution)/shard_map/all_to_all | solution.py:454
  62.9 0.9 shard_map.112
  63.7 3.8 %all-to-all-start.3 = ((f32[32,1,128]{2,1,0:T(1,128)}), f32[32,1,128]{2,1,0:T(1,128)S(1)}, u32[]{:S(2)}, u32[]{:S(2)}) async-start(f32[32,1,128]{2,1,0:T(1,128)} %get-tuple-element.44), calls=%async_computation.3 | async-start | bytes 32768 | tf_op jit(solution)/shard_map/all_to_all | solution.py:454
  67.6 4.6 %shard_map.113 = (f32[8,128]{1,0:T(8,128)S(1)}, f32[768,128]{1,0:T(8,128)S(1)}, f32[16,128]{1,0:T(8,128)S(1)}) custom-call(f32[928,128]{1,0:T(8,128)S(1)} %bitcast.11, f32[128,128]{1,0:T(8,128)S(1)} %bitcast.16, f32[16,128]{1,0:T(8,128)S(1)} %get-tuple-element.41.refs_2_.refs_4_), custom_call_target="tpu_custom_call" | custom-call | flops 30000000 | bytes 1048576 | tf_op jit(solution)/shard_map/pallas_call | solution.py:442
  72.1 3.9 %all-to-all-done.3 = f32[32,1,128]{2,1,0:T(1,128)S(1)} async-done(((f32[32,1,128]{2,1,0:T(1,128)}), f32[32,1,128]{2,1,0:T(1,128)S(1)}, u32[]{:S(2)}, u32[]{:S(2)}) %all-to-all-start.3) | async-done | bytes 16416 | tf_op jit(solution)/shard_map/all_to_all | solution.py:454
  76.1 0.4 shard_map.114
  76.5 11.7 %all_to_all.48.refs_0_ = f32[16,8,128]{2,1,0:T(8,128)S(1)} all-to-all(f32[16,8,128]{2,1,0:T(8,128)S(1)} %get-tuple-element.45), channel_id=1, replica_groups=mesh['x'=4,'z'=8,'core'=2,'narrow'=8] {'core','narrow'}, dimensions={0} | all-to-all | bytes 131072 | tf_op jit(solution)/shard_map/all_to_all | solution.py:454
  88.2 0.9 shard_map.115
  89.1 4.4 %all-to-all-start.5 = ((f32[32,1,128]{2,1,0:T(1,128)}), f32[32,1,128]{2,1,0:T(1,128)S(1)}, u32[]{:S(2)}, u32[]{:S(2)}) async-start(f32[32,1,128]{2,1,0:T(1,128)} %get-tuple-element.50), calls=%async_computation.5 | async-start | bytes 32768 | tf_op jit(solution)/shard_map/all_to_all | solution.py:454
  93.5 4.6 %shard_map.116 = (f32[8,128]{1,0:T(8,128)S(1)}, f32[768,128]{1,0:T(8,128)S(1)}, f32[16,128]{1,0:T(8,128)S(1)}) custom-call(f32[928,128]{1,0:T(8,128)S(1)} %bitcast.12, f32[128,128]{1,0:T(8,128)S(1)} %bitcast.18, f32[16,128]{1,0:T(8,128)S(1)} %get-tuple-element.41.refs_2_.refs_4_, f32[16,128]{1,0:T(8,128)S(1)} %get-tuple-element.47.refs_3_.refs_5_), custom_call_target="tpu_custom_call" | custom-call | flops 30000000 | bytes 1048576 | tf_op jit(solution)/shard_map/pallas_call | solution.py:442
  98.1 3.9 %all-to-all-done.5 = f32[32,1,128]{2,1,0:T(1,128)S(1)} async-done(((f32[32,1,128]{2,1,0:T(1,128)}), f32[32,1,128]{2,1,0:T(1,128)S(1)}, u32[]{:S(2)}, u32[]{:S(2)}) %all-to-all-start.5) | async-done | bytes 16416 | tf_op jit(solution)/shard_map/all_to_all | solution.py:454
  102.0 0.6 shard_map.117
  102.7 11.9 %all_to_all.49.refs_0_ = f32[16,8,128]{2,1,0:T(8,128)S(1)} all-to-all(f32[16,8,128]{2,1,0:T(8,128)S(1)} %get-tuple-element.52), channel_id=1, replica_groups=mesh['x'=4,'z'=8,'core'=2,'narrow'=8] {'core','narrow'}, dimensions={0} | all-to-all | bytes 131072 | tf_op jit(solution)/shard_map/all_to_all | solution.py:454
  114.6 0.9 shard_map.118
  115.4 4.7 %all-to-all-start.7 = ((f32[32,1,128]{2,1,0:T(1,128)}), f32[32,1,128]{2,1,0:T(1,128)S(1)}, u32[]{:S(2)}, u32[]{:S(2)}) async-start(f32[32,1,128]{2,1,0:T(1,128)} %get-tuple-element.57), calls=%async_computation.7 | async-start | bytes 32768 | tf_op jit(solution)/shard_map/all_to_all | solution.py:454
  120.2 4.7 %shard_map.119 = (f32[8,128]{1,0:T(8,128)S(1)}, f32[768,128]{1,0:T(8,128)S(1)}, f32[16,128]{1,0:T(8,128)S(1)}) custom-call(f32[928,128]{1,0:T(8,128)S(1)} %bitcast.13, f32[128,128]{1,0:T(8,128)S(1)} %bitcast.20, f32[16,128]{1,0:T(8,128)S(1)} %get-tuple-element.41.refs_2_.refs_4_, f32[16,128]{1,0:T(8,128)S(1)} %get-tuple-element.47.refs_3_.refs_5_, ...), custom_call_target="tpu_custom_call" | custom-call | flops 30000000 | bytes 1048576 | tf_op jit(solution)/shard_map/pallas_call | solution.py:442
  124.8 3.8 %all-to-all-done.7 = f32[32,1,128]{2,1,0:T(1,128)S(1)} async-done(((f32[32,1,128]{2,1,0:T(1,128)}), f32[32,1,128]{2,1,0:T(1,128)S(1)}, u32[]{:S(2)}, u32[]{:S(2)}) %all-to-all-start.7) | async-done | bytes 16416 | tf_op jit(solution)/shard_map/all_to_all | solution.py:454
  128.7 0.9 shard_map.120
  129.6 11.7 %all_to_all.50 = f32[16,1,128]{2,1,0:T(1,128)S(1)} all-to-all(f32[16,1,128]{2,1,0:T(1,128)S(1)} %shard_map.120), channel_id=1, replica_groups=mesh['x'=4,'z'=8,'core'=2,'narrow'=8] {'core','narrow'}, dimensions={0} | all-to-all | bytes 16384 | tf_op jit(solution)/shard_map/all_to_all | solution.py:454
  141.2 1.3 shard_map.121
Async XLA Ops:
  63.7 12.4 %all-to-all-start.3 = ((f32[32,1,128]{2,1,0:T(1,128)}), f32[32,1,128]{2,1,0:T(1,128)S(1)}, u32[]{:S(2)}, u32[]{:S(2)}) async-start(f32[32,1,128]{2,1,0:T(1,128)} %get-tuple-element.44), calls=%async_computation.3 | async-start | bytes 32768 | tf_op jit(solution)/shard_map/all_to_all | solution.py:454
  89.1 12.9 %all-to-all-start.5 = ((f32[32,1,128]{2,1,0:T(1,128)}), f32[32,1,128]{2,1,0:T(1,128)S(1)}, u32[]{:S(2)}, u32[]{:S(2)}) async-start(f32[32,1,128]{2,1,0:T(1,128)} %get-tuple-element.50), calls=%async_computation.5 | async-start | bytes 32768 | tf_op jit(solution)/shard_map/all_to_all | solution.py:454
  115.4 13.2 %all-to-all-start.7 = ((f32[32,1,128]{2,1,0:T(1,128)}), f32[32,1,128]{2,1,0:T(1,128)S(1)}, u32[]{:S(2)}, u32[]{:S(2)}) async-start(f32[32,1,128]{2,1,0:T(1,128)} %get-tuple-element.57), calls=%async_computation.7 | async-start | bytes 32768 | tf_op jit(solution)/shard_map/all_to_all | solution.py:454

commit v8 on v7

--- a/solution.py
+++ b/solution.py
@@ -18,7 +18,7 @@
 NROW = 16
 TARGETS = NROW * CAP
 GROUPS = TARGETS // 8
-BLOCK = 29
+BLOCK = 27
 AT_ONCE = 8
 LIST = TARGETS + 32
 
@@ -57,25 +57,30 @@
 
 def pack_kernel(*refs):
     block_out, row_out, state, *held = refs[7:17]
-    block, rows, sems = refs[17:]
+    moved, block, rows, sems = refs[17:]
     for copy in fetch(refs[:7], held, sems):
         copy.wait()
     pos, vel, acc, jerk, mass, levels, active = held
     for n, part in enumerate((pos, vel, acc, jerk)):
         state[3 * n : 3 * n + 3, :] = part[...]
     times = step_size * (1.0 - jnp.left_shift(1, levels[...]).astype(jnp.float32))
-    state[12:15, :] = jnp.broadcast_to(times, (3, STARS))
-    state[15:16, :] = mass[...]
-    whole = state[...]
+    state[12:16, :] = jnp.zeros((4, STARS), jnp.float32)
+    tau = step_size - times
+    x, v = predict(pos[...], vel[...], acc[...], jerk[...], tau)
+    for n, part in enumerate((x, v, acc[...] + tau * jerk[...], jerk[...])):
+        moved[3 * n : 3 * n + 3, :] = part
+    moved[12:15, :] = jnp.broadcast_to(times, (3, STARS))
+    moved[15:16, :] = mass[...]
+    whole = moved[...]
     lane = lane_of((1, LANES))
     names = jnp.full((1, LANES), STARS, jnp.int32)
     for k in range(STEPS):
         for s in range(CAP):
             names = jnp.where(lane == CAP * k + s, active[k, s], names)
     for h in range(2):
-        block[14 * h : 14 * h + 13, :] = whole[0:13, LANES * h : LANES * h + LANES]
-        block[14 * h + 13 : 14 * h + 14, :] = whole[15:16, LANES * h : LANES * h + LANES]
-    block[28:29, :] = names.astype(jnp.float32)
+        block[13 * h : 13 * h + 12, :] = whole[0:12, LANES * h : LANES * h + LANES]
+        block[13 * h + 12 : 13 * h + 13, :] = whole[15:16, LANES * h : LANES * h + LANES]
+    block[26:27, :] = names.astype(jnp.float32)
     filled = block[0:BLOCK, :]
     for p in range(block_out.shape[0] // BLOCK):
         block_out[BLOCK * p : BLOCK * p + BLOCK, :] = filled
@@ -126,9 +131,9 @@
         at = pl.ds(h * ncol, ncol)
 
         def load(q):
-            return raw[pl.ds(14 * h + q, ncol, stride=BLOCK), :]
-
-        tau = block_time - load(12)
+            return raw[pl.ds(13 * h + q, ncol, stride=BLOCK), :]
+
+        tau = block_time - step_size
         for c in range(3):
             x, v = predict(load(c), load(3 + c), load(6 + c), load(9 + c), tau)
             source[c, at, :] = x
@@ -136,7 +141,8 @@
 
 
 def spread_targets(z, splat, block_time):
-    x, v = predict(z, back(z, 24), back(z, 48), back(z, 72), block_time - back(z, 96))
+    tau = block_time - jnp.maximum(back(z, 96), step_size)
+    x, v = predict(z, back(z, 24), back(z, 48), back(z, 72), tau)
     for q in range(6):
         held = x if q < 3 else v
         for s in range(CAP):
@@ -209,7 +215,7 @@
 
 
 def load_masses(raw, ncol):
-    return [raw[pl.ds(14 * h + 13, ncol, stride=BLOCK), :] for h in range(2)]
+    return [raw[pl.ds(13 * h + 12, ncol, stride=BLOCK), :] for h in range(2)]
 
 
 def first_force_kernel(ncol, raw, target_rows, sums_out, *work):
@@ -249,7 +255,7 @@
     spread_targets(rows, splat, block_time)
     predict_sources(raw, source, block_time, ncol)
     masses = load_masses(raw, ncol)
-    names = raw[pl.ds(28, ncol, stride=BLOCK), :]
+    names = raw[pl.ds(26, ncol, stride=BLOCK), :]
     lane = lane_of((ncol, LANES)).astype(jnp.float32)
     for at in range(CAP * step):
         named = jnp.broadcast_to(names[:, at : at + 1], (ncol, LANES))
@@ -346,9 +352,12 @@
 def correct_rows(step, total, z, names):
     block_time = (step + 1) * step_size
     lane = lane_of(z.shape)
-    tau = block_time - back(z, 96)
-    old_acc, old_jerk = back(z, 48), back(z, 72)
-    x, v = predict(z, back(z, 24), old_acc, old_jerk, tau)
+    times = back(z, 96)
+    held_at = jnp.maximum(times, step_size)
+    held_acc, old_jerk = back(z, 48), back(z, 72)
+    x, v = predict(z, back(z, 24), held_acc, old_jerk, block_time - held_at)
+    old_acc = held_acc - (held_at - times) * old_jerk
+    tau = block_time - times
     new_a, new_j = total, back(total, 24)
     pos_step, vel_step = correct(old_acc, old_jerk, new_a, new_j, tau)
 
@@ -475,7 +484,8 @@
         [scratch(3, STARS)] * 4
         + [scratch(1, STARS), pltpu.VMEM((1, STARS), jnp.int32)]
         + [pltpu.SMEM((STEPS, CAP), jnp.int32)]
-        + [scratch(32, LANES), scratch(8, LANES), pltpu.SemaphoreType.DMA((7,))],
+        + [scratch(16, STARS), scratch(32, LANES), scratch(8, LANES)]
+        + [pltpu.SemaphoreType.DMA((7,))],
         [hbm] * 7,
     )
     target_rows = send_all(rows, row_axes).reshape(NROW * 8, LANES)

time: 143 us -> 143 us (level)
  waiting for transfers between devices: 11.7 us -> 9.96 us
    all_to_all x3, waiting for transfers between devices: 11.7 us -> 9.96 us  [send_all(): return lax.all_to_all(x, axes, split_axis=0, concat_axis=0, tiled=True)]
  transfers between devices with their start and end apart: 3 -> 3, of which waited for: 3 -> 3; matrix products, arithmetic and copies ran while one was open for 0% -> 0% of each run, Pallas kernels for 10% -> 11%
where the time goes in v8:
time: 143 us; the launch traced here: 142 us
  blocking collectives  90.7 us (63%)
  Pallas kernels  27.4 us (19%)
  starting transfers between devices  13.6 us (10%)
  waiting for transfers between devices  9.96 us (7%)
    all_to_all x6, blocking collectives, send_all(): return lax.all_to_all(x, axes, split_axis=0, concat_axis=0, tiled=True)  90.7 us
    pallas_call x12, Pallas kernels, call(): pl.pallas_call(kernel, out_shape=tuple(outs), in_specs=specs or [vmem] *...  27.4 us
    all_to_all x3, starting transfers between devices, send_all(): return lax.all_to_all(x, axes, split_axis=0, concat_axis=0, tiled=True)  13.6 us
    all_to_all x3, waiting for transfers between devices, send_all(): return lax.all_to_all(x, axes, split_axis=0, concat_axis=0, tiled=True)  9.96 us
  transfers between devices with their start and end apart: 3, of which 3 were waited for; matrix products, arithmetic and copies ran while one was open for 0% of the time, Pallas kernels for 11%

profile of v8, /device:TPU:1, one launch (start us, length us, event | category | flops | bytes accessed | tf_op | source)
XLA Modules:
  0.0 142.4 jit_solution(2996397645735258166)
XLA Ops:
  0.6 1.1 shard_map.110
  1.7 16.5 %all_to_all.45 = f32[16,8,128]{2,1,0:T(8,128)S(1)} all-to-all(f32[16,8,128]{2,1,0:T(8,128)S(1)} %get-tuple-element.38), channel_id=1, replica_groups=mesh['x'=4,'z'=8,'core'=2,'narrow'=8] {'core','narrow'}, dimensions={0} | all-to-all | bytes 131072 | tf_op jit(solution)/shard_map/all_to_all | solution.py:463
  18.2 26.0 %all_to_all.46 = f32[32,1,3456]{2,1,0:T(1,128)S(1)} all-to-all(f32[32,1,3456]{2,1,0:T(1,128)S(1)} %bitcast.22), channel_id=1, replica_groups=mesh['x'=4,'z'=8,'core'=2,'narrow'=8] {'z','x'}, dimensions={0} | all-to-all | bytes 884736 | tf_op jit(solution)/shard_map/all_to_all | solution.py:463
  44.2 5.0 %shard_map.111 = f32[16,8,128]{2,1,0:T(8,128)S(1)} custom-call(f32[864,128]{1,0:T(8,128)S(1)} %bitcast.10, f32[128,128]{1,0:T(8,128)S(1)} %bitcast.14), custom_call_target="tpu_custom_call" | custom-call | tf_op jit(solution)/shard_map/pallas_call | solution.py:451
  49.2 12.7 %all_to_all.47.refs_0_ = f32[16,8,128]{2,1,0:T(8,128)S(1)} all-to-all(f32[16,8,128]{2,1,0:T(8,128)S(1)} %shard_map.111), channel_id=1, replica_groups=mesh['x'=4,'z'=8,'core'=2,'narrow'=8] {'core','narrow'}, dimensions={0} | all-to-all | bytes 131072 | tf_op jit(solution)/shard_map/all_to_all | solution.py:463
  61.9 0.9 shard_map.112
  62.7 4.1 %all-to-all-start.3 = ((f32[32,1,128]{2,1,0:T(1,128)}), f32[32,1,128]{2,1,0:T(1,128)S(1)}, u32[]{:S(2)}, u32[]{:S(2)}) async-start(f32[32,1,128]{2,1,0:T(1,128)} %get-tuple-element.44), calls=%async_computation.3 | async-start | bytes 32768 | tf_op jit(solution)/shard_map/all_to_all | solution.py:463
  66.8 5.0 %shard_map.113 = (f32[8,128]{1,0:T(8,128)S(1)}, f32[768,128]{1,0:T(8,128)S(1)}, f32[16,128]{1,0:T(8,128)S(1)}) custom-call(f32[864,128]{1,0:T(8,128)S(1)} %bitcast.11, f32[128,128]{1,0:T(8,128)S(1)} %bitcast.16, f32[16,128]{1,0:T(8,128)S(1)} %get-tuple-element.41.refs_2_.refs_4_), custom_call_target="tpu_custom_call" | custom-call | flops 30000000 | bytes 1048576 | tf_op jit(solution)/shard_map/pallas_call | solution.py:451
  71.9 3.5 %all-to-all-done.3 = f32[32,1,128]{2,1,0:T(1,128)S(1)} async-done(((f32[32,1,128]{2,1,0:T(1,128)}), f32[32,1,128]{2,1,0:T(1,128)S(1)}, u32[]{:S(2)}, u32[]{:S(2)}) %all-to-all-start.3) | async-done | bytes 16416 | tf_op jit(solution)/shard_map/all_to_all | solution.py:463
  75.4 0.4 shard_map.114
  75.8 11.9 %all_to_all.48.refs_0_ = f32[16,8,128]{2,1,0:T(8,128)S(1)} all-to-all(f32[16,8,128]{2,1,0:T(8,128)S(1)} %get-tuple-element.45), channel_id=1, replica_groups=mesh['x'=4,'z'=8,'core'=2,'narrow'=8] {'core','narrow'}, dimensions={0} | all-to-all | bytes 131072 | tf_op jit(solution)/shard_map/all_to_all | solution.py:463
  87.7 0.9 shard_map.115
  88.6 4.6 %all-to-all-start.5 = ((f32[32,1,128]{2,1,0:T(1,128)}), f32[32,1,128]{2,1,0:T(1,128)S(1)}, u32[]{:S(2)}, u32[]{:S(2)}) async-start(f32[32,1,128]{2,1,0:T(1,128)} %get-tuple-element.50), calls=%async_computation.5 | async-start | bytes 32768 | tf_op jit(solution)/shard_map/all_to_all | solution.py:463
  93.2 5.0 %shard_map.116 = (f32[8,128]{1,0:T(8,128)S(1)}, f32[768,128]{1,0:T(8,128)S(1)}, f32[16,128]{1,0:T(8,128)S(1)}) custom-call(f32[864,128]{1,0:T(8,128)S(1)} %bitcast.12, f32[128,128]{1,0:T(8,128)S(1)} %bitcast.18, f32[16,128]{1,0:T(8,128)S(1)} %get-tuple-element.41.refs_2_.refs_4_, f32[16,128]{1,0:T(8,128)S(1)} %get-tuple-element.47.refs_3_.refs_5_), custom_call_target="tpu_custom_call" | custom-call | flops 30000000 | bytes 1048576 | tf_op jit(solution)/shard_map/pallas_call | solution.py:451
  98.2 3.5 %all-to-all-done.5 = f32[32,1,128]{2,1,0:T(1,128)S(1)} async-done(((f32[32,1,128]{2,1,0:T(1,128)}), f32[32,1,128]{2,1,0:T(1,128)S(1)}, u32[]{:S(2)}, u32[]{:S(2)}) %all-to-all-start.5) | async-done | bytes 16416 | tf_op jit(solution)/shard_map/all_to_all | solution.py:463
  101.7 0.6 shard_map.117
  102.3 11.9 %all_to_all.49.refs_0_ = f32[16,8,128]{2,1,0:T(8,128)S(1)} all-to-all(f32[16,8,128]{2,1,0:T(8,128)S(1)} %get-tuple-element.52), channel_id=1, replica_groups=mesh['x'=4,'z'=8,'core'=2,'narrow'=8] {'core','narrow'}, dimensions={0} | all-to-all | bytes 131072 | tf_op jit(solution)/shard_map/all_to_all | solution.py:463
  114.3 0.9 shard_map.118
  115.1 4.9 %all-to-all-start.7 = ((f32[32,1,128]{2,1,0:T(1,128)}), f32[32,1,128]{2,1,0:T(1,128)S(1)}, u32[]{:S(2)}, u32[]{:S(2)}) async-start(f32[32,1,128]{2,1,0:T(1,128)} %get-tuple-element.57), calls=%async_computation.7 | async-start | bytes 32768 | tf_op jit(solution)/shard_map/all_to_all | solution.py:463
  120.0 5.5 %shard_map.119 = (f32[8,128]{1,0:T(8,128)S(1)}, f32[768,128]{1,0:T(8,128)S(1)}, f32[16,128]{1,0:T(8,128)S(1)}) custom-call(f32[864,128]{1,0:T(8,128)S(1)} %bitcast.13, f32[128,128]{1,0:T(8,128)S(1)} %bitcast.20, f32[16,128]{1,0:T(8,128)S(1)} %get-tuple-element.41.refs_2_.refs_4_, f32[16,128]{1,0:T(8,128)S(1)} %get-tuple-element.47.refs_3_.refs_5_, ...), custom_call_target="tpu_custom_call" | custom-call | flops 30000000 | bytes 1048576 | tf_op jit(solution)/shard_map/pallas_call | solution.py:451
  125.5 3.0 %all-to-all-done.7 = f32[32,1,128]{2,1,0:T(1,128)S(1)} async-done(((f32[32,1,128]{2,1,0:T(1,128)}), f32[32,1,128]{2,1,0:T(1,128)S(1)}, u32[]{:S(2)}, u32[]{:S(2)}) %all-to-all-start.7) | async-done | bytes 16416 | tf_op jit(solution)/shard_map/all_to_all | solution.py:463
  128.5 0.9 shard_map.120
  129.4 11.7 %all_to_all.50 = f32[16,1,128]{2,1,0:T(1,128)S(1)} all-to-all(f32[16,1,128]{2,1,0:T(1,128)S(1)} %shard_map.120), channel_id=1, replica_groups=mesh['x'=4,'z'=8,'core'=2,'narrow'=8] {'core','narrow'}, dimensions={0} | all-to-all | bytes 16384 | tf_op jit(solution)/shard_map/all_to_all | solution.py:463
  141.1 1.3 shard_map.121
Async XLA Ops:
  62.7 12.6 %all-to-all-start.3 = ((f32[32,1,128]{2,1,0:T(1,128)}), f32[32,1,128]{2,1,0:T(1,128)S(1)}, u32[]{:S(2)}, u32[]{:S(2)}) async-start(f32[32,1,128]{2,1,0:T(1,128)} %get-tuple-element.44), calls=%async_computation.3 | async-start | bytes 32768 | tf_op jit(solution)/shard_map/all_to_all | solution.py:463
  88.6 13.1 %all-to-all-start.5 = ((f32[32,1,128]{2,1,0:T(1,128)}), f32[32,1,128]{2,1,0:T(1,128)S(1)}, u32[]{:S(2)}, u32[]{:S(2)}) async-start(f32[32,1,128]{2,1,0:T(1,128)} %get-tuple-element.50), calls=%async_computation.5 | async-start | bytes 32768 | tf_op jit(solution)/shard_map/all_to_all | solution.py:463
  115.1 13.4 %all-to-all-start.7 = ((f32[32,1,128]{2,1,0:T(1,128)}), f32[32,1,128]{2,1,0:T(1,128)S(1)}, u32[]{:S(2)}, u32[]{:S(2)}) async-start(f32[32,1,128]{2,1,0:T(1,128)} %get-tuple-element.57), calls=%async_computation.7 | async-start | bytes 32768 | tf_op jit(solution)/shard_map/all_to_all | solution.py:463
